TPU v7x, 32 devices: a whole 2x2x4 slice. The times are simulated.
32 devices in a mesh: parts: 2 (over y), att: 4 (over x, core), ffn: 4 (over z).
Axes of the slice: x: 2, y: 2, z: 4, core: 2. Of those that a mesh axis runs over, the one named last changes fastest.
Arguments:
- incoming: bfloat16 [128, 2, 8192], P('parts', None, 'att'), parts along dimension 0, may hold values from -60 to 60
- queries: bfloat16 [128, 2, 8192], P(('parts', 'att'), None, 'ffn'), parts along dimension 0, may hold values from -19 to 19
- new_kv: bfloat16 [128, 2, 2048], P(('parts', 'att'), None, 'ffn'), parts along dimension 0, may hold values from -6 to 6
- cache: bfloat16 [128, 640, 2048], P(('parts', 'att'), None, 'ffn'), parts along dimension 0, may hold values from -6 to 6
- lengths: int32 [128], P(('parts', 'att')), parts along dimension 0, may hold values from 1 to 640, 20480 in all
- slot_of: int32 [128], P('parts'), parts along dimension 0, may hold values from 0 to 63, each once
- w_out: bfloat16 [8192, 8192], P('ffn', 'att'), may hold values from -0.0625 to 0.0625
- norm_gain: float32 [8192], P('att'), may hold values from 0.5 to 1.5
- w_gate: bfloat16 [8192, 14336], P('att', 'ffn'), may hold values from -0.0625 to 0.0625
- w_up: bfloat16 [8192, 14336], P('att', 'ffn'), may hold values from -0.0625 to 0.0625
- w_down: bfloat16 [14336, 8192], P('ffn', 'att'), may hold values from -0.046875 to 0.046875
Outputs:
- out: bfloat16 [128, 2, 8192], P(('parts', 'ffn'), None, 'att'), parts along dimension 0
There are 2 independent parts, one for each index of `parts`. A program takes and returns all parts, laid end to end along the dimension named above; an argument that names none is the same for every part. Nothing has to cross between parts.
Inputs may be any that keep to these rules, and one draw needn't show every extreme that they name: In each part, the kept lengths of that part's 64 slots sum to 20480. `slot_of`: in each part, every slot holds exactly one request.
All inputs are finite; a program needn't handle non-finite values. No bound on the sum of `lengths` on one device may be relied on, other than what follows from the above.
Results may differ from a plain program's by a relative error of at most 0.0095.
Values may be sent and summed in bfloat16 or wider, within the bound.
No kernel may reach another device: no remote copies, remote signals or barrier semaphores. Data moves between devices by JAX's collectives and lax.ppermute only.
A program may use at most 128 MiB of HBM per device.

v0:
```python
import functools

import jax
import jax.numpy as jnp
from jax import lax
from jax.experimental import pallas as pl
from jax.experimental.pallas import tpu as pltpu
from jax.sharding import PartitionSpec as P

H = 64
KVH = 8
HD = 128
STEPS = 2
GROUPS = H // KVH
EPSILON = 1e-05
BLOCK = 256
CHUNKS = (2, 3, 2)
WAIT = 2 * 10**9
F32 = jnp.float32
BF16 = jnp.bfloat16
MIB = 1024 * 1024


def dot(a, b):
    return jnp.dot(a, b, preferred_element_type=F32)

VMEM = pl.BlockSpec(memory_space=pltpu.VMEM)
ANY = pl.BlockSpec(memory_space=pl.ANY)


def shift(x, axis, d):
    n = lax.axis_size(axis)
    return lax.ppermute(x, axis, [(i, (i + d) % n) for i in range(n)])


def exchange(x, axis, bit):
    return lax.ppermute(x, axis, [(i, i ^ bit) for i in range(lax.axis_size(axis))])


def corner(x):
    return x[:8, :HD]


def limit(mib):
    return pltpu.CompilerParams(vmem_limit_bytes=mib * MIB)


def join(blocks, after=()):
    count = len(blocks)
    rows = [block.shape[0] for block in blocks]

    def kernel(*refs):
        out, at = refs[-1], 0
        for ref, size in zip(refs[:count], rows):
            out[at : at + size, :] = ref[...]
            at += size

    return pl.pallas_call(
        kernel,
        name="join",
        out_shape=jax.ShapeDtypeStruct((sum(rows), blocks[0].shape[1]), blocks[0].dtype),
        in_specs=[VMEM] * (count + len(after)),
        out_specs=VMEM,
        compiler_params=limit(4),
    )(*blocks, *after)


def gather_att(x, token=()):
    chips = lax.axis_size("att") // 2
    same = join([x] + [shift(x, "att", 2 * d) for d in range(1, chips)], token)
    return same, exchange(same, "att", 1)


def place_gathered(same, other, whole, columns=slice(None)):
    me, chips = lax.axis_index("att"), lax.axis_size("att") // 2
    rows = same.shape[0] // chips
    for d in range(chips):
        chip = lax.rem(me // 2 + chips - d, chips)
        for side, ref in enumerate((same, other)):
            source = chip * 2 + lax.rem(me + side, 2)
            at = pl.multiple_of(source * rows, rows)
            whole[pl.ds(at, rows), columns] = ref[d * rows : (d + 1) * rows, :]


def reduce_ffn(own, near, keep, far, *ahead):
    direct = [exchange(rows, "ffn", k + 2) for k, rows in enumerate(ahead)]
    sums = add_parts(keep, exchange(far, "ffn", 1), len(ahead) // 2)
    across = [exchange(part, "ffn", 2 * (k + 1)) for k, part in enumerate(sums)]
    return [own, *direct, *across, exchange(near, "ffn", 1)]


def add_terms(refs, columns):
    own, rest, near = refs[0], refs[1:-1], refs[-1]
    half = own.shape[1] // 2
    direct = 2 * len(rest) // 3
    left = columns.stop <= half
    total = own[:, columns] + near[:, columns].astype(F32)
    here = columns if left else slice(columns.start - half, columns.stop - half)
    for term in rest[:direct] if left else rest[direct:]:
        total = total + term[:, here].astype(F32)
    return total


def gather_ffn(x, left, right):
    ffn, half = lax.axis_size("ffn"), left.shape[1]
    blocks = [(1, 0, exchange(x, "ffn", 1))]
    for mask in range(2, ffn, 2):
        moved = exchange(right, "ffn", mask)
        blocks += [(mask + 1, half, exchange(moved, "ffn", 1)), (mask, half, moved)]
    blocks += [(mask, 0, exchange(left, "ffn", mask)) for mask in range(ffn - 1, 1, -1)]
    return blocks + [(0, 0, x)]


def vmem(x):
    return pltpu.with_memory_space_constraint(x, pltpu.VMEM)


def hbm(x):
    return pltpu.with_memory_space_constraint(x, pltpu.HBM)


class Copies:
    def __init__(self, entries):
        self.entries = entries
        self.sources = [hbm(x) for x, _ in entries]
        self.shapes = [pltpu.VMEM((n,) + x.shape[1:], x.dtype) for x, n in entries]
        self.scratch = pltpu.SemaphoreType.DMA((len(entries), 8))
        self.bytes = sum(2 * x.size // x.shape[0] * n * x.dtype.itemsize for x, n in entries)

    def started(self, sources, targets, sems):
        copies = []
        for k, (x, rows) in enumerate(self.entries):
            parts = 8 if rows % 8 == 0 and x.size >= MIB else 1
            size = rows // parts
            begin = 0 if rows == x.shape[0] else lax.axis_index("ffn") * rows
            for p in range(parts):
                copies.append(
                    pltpu.make_async_copy(
                        sources[k].at[pl.ds(begin + p * size, size)],
                        targets[k].at[pl.ds(p * size, size)],
                        sems.at[k, p],
                    )
                )
        for copy in copies:
            copy.start()
        return copies


def load(entries, name, after=()):
    work = Copies(entries)
    count = len(entries)

    def kernel(*refs):
        targets, token, sems = refs[-2 - count : -2], refs[-2], refs[-1]
        copies = work.started(refs[:count], targets, sems)
        token[...] = jnp.zeros_like(token)
        for copy in copies:
            copy.wait()

    return pl.pallas_call(
        kernel,
        name=name,
        out_shape=work.shapes + [jax.ShapeDtypeStruct((8, HD), F32)],
        in_specs=[ANY] * count + [VMEM] * len(after),
        out_specs=[VMEM] * (count + 1),
        scratch_shapes=[work.scratch],
        compiler_params=limit(1),
        cost_estimate=pl.CostEstimate(flops=0, bytes_accessed=work.bytes, transcendentals=0),
    )(*work.sources, *after)


def attend(lengths, slot_row, same, other, cache):
    slots, cap, width = cache.shape
    kv_local = width // (2 * HD)
    heads = kv_local * GROUPS
    rows = STEPS * heads
    requests = slot_row.shape[1]
    fresh_at = STEPS * heads * HD
    columns = fresh_at + STEPS * width
    factor = HD ** (-0.5) * 1.4426950408889634

    def kernel(lengths, slot_row, same, other, cache, out, *scratch):
        qkv, qs, fresh, wide, scores, fresh_scores, mixed = scratch
        place_gathered(same, other, qkv)
        base = lax.axis_index("att") * slots
        wanted = lax.broadcasted_iota(jnp.int32, (slots, requests), 0) + base
        pick = jnp.where(slot_row[...] == wanted, 1.0, 0.0).astype(BF16)
        mine = dot(pick, qkv[...])
        for s in range(STEPS):
            for h in range(heads):
                at = (s * heads + h) * HD
                qs[pl.ds(s * heads + h, slots, stride=rows), :] = mine[:, at : at + HD]
            fresh[s * slots : (s + 1) * slots, :] = mine[
                :, fresh_at + s * width : fresh_at + (s + 1) * width
            ].astype(BF16)
        group_of = lax.broadcasted_iota(jnp.int32, (slots * rows, HD), 0) % heads // GROUPS
        for g in range(kv_local):
            own = jnp.where(group_of == g, qs[...], 0.0)
            wide[:, g * HD : (g + 1) * HD] = own.astype(BF16)

        def of_groups(rows_kept, which):
            at = [g * 2 * HD + which * HD for g in range(kv_local)]
            return jnp.concatenate([rows_kept[:, first : first + HD] for first in at], axis=1)

        across = (((1,), (1,)), ((), ()))
        fresh_scores[...] = lax.dot_general(
            wide[...], of_groups(fresh, 0), across, preferred_element_type=F32
        )
        for i in range(slots):
            here = slice(i * rows, (i + 1) * rows)
            scores[here, :] = lax.dot_general(
                wide[here, :], of_groups(cache.at[i], 0), across, preferred_element_type=F32
            )
        key_at = lax.broadcasted_iota(jnp.int32, (rows, cap), 1)
        fresh_step = lax.broadcasted_iota(jnp.int32, (rows, STEPS * slots), 1)
        row_step = lax.broadcasted_iota(jnp.int32, (rows, STEPS * slots), 0) // heads
        for i in range(slots):
            here = slice(i * rows, (i + 1) * rows)
            kept = jnp.where(key_at < lengths[:, i : i + 1], scores[here, :], -jnp.inf)
            own = (fresh_step % slots == i) & (fresh_step // slots <= row_step)
            new = jnp.where(own, fresh_scores[here, :], -jnp.inf)
            top = jnp.maximum(
                jnp.max(kept, axis=1, keepdims=True), jnp.max(new, axis=1, keepdims=True)
            )
            kept = jnp.exp2((kept - top) * factor)
            new = jnp.exp2((new - top) * factor)
            total = jnp.sum(kept, axis=1, keepdims=True) + jnp.sum(new, axis=1, keepdims=True)
            values = dot(kept.astype(BF16), of_groups(cache.at[i], 1))
            values = values + dot(new.astype(BF16), of_groups(fresh, 1))
            values = values / total
            for s in range(STEPS):
                for g in range(kv_local):
                    at = s * heads + g * GROUPS
                    mixed[i * rows + at : i * rows + at + GROUPS, :] = values[
                        at : at + GROUPS, g * HD : (g + 1) * HD
                    ]
        for s in range(STEPS):
            for h in range(heads):
                out[s * slots : (s + 1) * slots, h * HD : (h + 1) * HD] = mixed[
                    pl.ds(s * heads + h, slots, stride=rows), :
                ].astype(BF16)
    return pl.pallas_call(
        kernel,
        name="attend",
        out_shape=jax.ShapeDtypeStruct((STEPS * slots, heads * HD), BF16),
        in_specs=[VMEM] * 5,
        out_specs=VMEM,
        scratch_shapes=[
            pltpu.VMEM((requests, columns), BF16),
            pltpu.VMEM((slots * rows, HD), F32),
            pltpu.VMEM((STEPS * slots, width), BF16),
            pltpu.VMEM((slots * rows, kv_local * HD), BF16),
            pltpu.VMEM((slots * rows, cap), F32),
            pltpu.VMEM((slots * rows, STEPS * slots), F32),
            pltpu.VMEM((slots * rows, HD), F32),
        ],
        compiler_params=limit(6),
        cost_estimate=pl.CostEstimate(
            flops=4 * slots * rows * cap * width,
            bytes_accessed=slots * cap * width * 2,
            transcendentals=slots * rows * cap,
        ),
    )(lengths, slot_row, same, other, cache)


def matmul_cost(rows, depth, columns):
    return pl.CostEstimate(
        flops=2 * rows * depth * columns,
        bytes_accessed=2 * (rows * depth + depth * columns + rows * columns),
        transcendentals=0,
    )


def order_rows(slot_row, same, other):
    requests = slot_row.shape[1]
    rows = STEPS * requests
    depth = same.shape[1]
    slots = requests // lax.axis_size("att")
    ffn = lax.axis_size("ffn")
    owned = requests // ffn

    def kernel(slot_row, same, other, out, gathered, natural):
        place_gathered(same, other, gathered)
        slot = slot_row[...]
        first = lax.div(slot, slots) * (STEPS * slots) + lax.rem(slot, slots)
        at = lax.broadcasted_iota(jnp.int32, (rows, requests), 0)
        me = lax.axis_index("ffn")
        for step in range(STEPS):
            pick = jnp.where(at == first + step * slots, 1.0, 0.0).astype(BF16)
            picked = lax.dot_general(
                pick, gathered[...], (((0,), (0,)), ((), ())), preferred_element_type=F32
            )
            natural[...] = picked.astype(BF16)
            for r in range(ffn):
                owner = jnp.bitwise_xor(me, r)
                here = slice((r * STEPS + step) * owned, (r * STEPS + step + 1) * owned)
                out[here, :] = natural[pl.ds(pl.multiple_of(owner * owned, owned), owned), :]

    return pl.pallas_call(
        kernel,
        name="order_rows",
        out_shape=jax.ShapeDtypeStruct((rows, depth), BF16),
        in_specs=[VMEM] * 3,
        out_specs=VMEM,
        scratch_shapes=[pltpu.VMEM((rows, depth), BF16), pltpu.VMEM((requests, depth), BF16)],
        compiler_params=limit(4),
    )(slot_row, same, other)


def multiply(rows, w, name):
    columns = w.shape[1]
    half = columns // 2
    count, depth = rows.shape
    ffn = lax.axis_size("ffn")
    share = count // ffn
    rest = (ffn // 2 - 1) * share
    block = min(512, half)

    def kernel(rows, w, own, near, keep, far, *ahead):
        for at in range(0, columns, block):
            here = slice(at, at + block)
            product = dot(rows[...], w[:, here])
            own[:, here] = product[:share]
            near[:, here] = product[share : 2 * share].astype(BF16)
            for r in range(2, ffn):
                part = product[r * share : (r + 1) * share]
                if at < half:
                    ahead[r - 2][:, here] = part.astype(BF16)
                else:
                    out = far if r % 2 else keep
                    place = slice((r // 2 - 1) * share, r // 2 * share)
                    out[place, at - half : at - half + block] = part.astype(out.dtype)

    return pl.pallas_call(
        kernel,
        name=name,
        out_shape=[
            jax.ShapeDtypeStruct((share, columns), F32),
            jax.ShapeDtypeStruct((share, columns), BF16),
            jax.ShapeDtypeStruct((rest, half), F32),
            jax.ShapeDtypeStruct((rest, half), BF16),
        ]
        + [jax.ShapeDtypeStruct((share, half), BF16)] * (ffn - 2),
        in_specs=[VMEM] * 2,
        out_specs=[VMEM] * (ffn + 2),
        compiler_params=limit(4),
        cost_estimate=matmul_cost(count, depth, columns),
    )(rows, vmem(w))


def add_parts(keep, arrived, parts, first=BF16):
    rows, width = keep.shape
    share = rows // parts
    types = [first] + [BF16] * (parts - 1)

    def kernel(keep, arrived, *outs):
        for d, out in enumerate(outs):
            here = slice(d * share, (d + 1) * share)
            out[...] = (keep[here, :].astype(F32) + arrived[here, :].astype(F32)).astype(out.dtype)

    return pl.pallas_call(
        kernel,
        name="add_parts",
        out_shape=[jax.ShapeDtypeStruct((share, width), kind) for kind in types],
        in_specs=[VMEM] * 2,
        out_specs=[VMEM] * parts,
        compiler_params=limit(4),
    )(keep, arrived)


def add_residual(own, terms):
    rows, columns = terms[0].shape
    owned, half = rows // STEPS, columns // 2

    def kernel(own, *refs):
        terms, (whole, left, right) = refs[:-3], refs[-3:]
        for out, first in ((left, 0), (right, half)):
            total = add_terms(terms, slice(first, first + half))
            for step in range(STEPS):
                here = slice(step * owned, (step + 1) * owned)
                at = step * columns + first
                value = (own[:, at : at + half].astype(F32) + total[here]).astype(BF16)
                out[here, :] = value
                whole[here, first : first + half] = value

    return pl.pallas_call(
        kernel,
        name="add_residual",
        out_shape=[jax.ShapeDtypeStruct((rows, n), BF16) for n in (columns, half, half)],
        in_specs=[VMEM] * (1 + len(terms)),
        out_specs=[VMEM] * 3,
        compiler_params=limit(4),
    )(own, *terms)


def norm_rows(blocks, gain):
    places = [(mask, first) for mask, first, _ in blocks]
    flat = [block for _, _, block in blocks]
    size, depth = flat[-1].shape
    rows = size * lax.axis_size("ffn")
    att = lax.axis_size("att")
    chips = att // 2
    share = rows // att

    def kernel(*refs):
        blocks, (gain, normed, tail, residual) = refs[: len(flat)], refs[len(flat) :]
        for (mask, first), block in zip(places, blocks):
            here = slice(first, first + block.shape[1])
            residual[mask * size : (mask + 1) * size, here] = block[...]
        me = lax.axis_index("att")
        chip, core = me // 2, lax.rem(me, 2)
        for side in range(2):
            for d in range(chips):
                owner = lax.rem(chip + d, chips) * 2 + lax.rem(core + side, 2)
                part = residual[pl.ds(pl.multiple_of(owner * share, share), share), :].astype(F32)
                here = slice((side * chips + d) * share, (side * chips + d + 1) * share)
                normed[here, :] = (part * gain[...]).astype(BF16)
                squares = jnp.sum(part * part, axis=1, keepdims=True)
                high = squares.astype(BF16).astype(F32)
                lane = lax.broadcasted_iota(jnp.int32, (share, HD), 1)
                tail[here, :] = jnp.where(lane == 0, high, squares - high).astype(BF16)

    return pl.pallas_call(
        kernel,
        name="norm_rows",
        out_shape=[
            jax.ShapeDtypeStruct((rows, depth), BF16),
            jax.ShapeDtypeStruct((rows, HD), BF16),
        ],
        in_specs=[VMEM] * (len(flat) + 1),
        out_specs=[VMEM] * 2,
        scratch_shapes=[pltpu.VMEM((rows, depth), BF16)],
        compiler_params=limit(4),
    )(*flat, gain)


def widen(normed, tail, w_gate, w_up, first, count, after):
    rows, depth = normed.shape
    half = rows // 2
    width = count * 2 * BLOCK + HD

    def kernel(normed, tail, gate, up, *refs):
        keep, send = refs[-2:]
        keep[:, count * 2 * BLOCK :] = tail[:half, :]
        send[:, count * 2 * BLOCK :] = tail[half:, :]
        for j in range(count):
            for which, w in enumerate((gate, up)):
                at = (first + j) * BLOCK
                product = dot(normed[...], w[:, at : at + BLOCK])
                here = slice((2 * j + which) * BLOCK, (2 * j + which + 1) * BLOCK)
                keep[:, here] = product[:half].astype(BF16)
                send[:, here] = product[half:].astype(BF16)

    return pl.pallas_call(
        kernel,
        name="widen",
        out_shape=[jax.ShapeDtypeStruct((half, width), BF16)] * 2,
        in_specs=[VMEM] * (4 + len(after)),
        out_specs=[VMEM] * 2,
        compiler_params=limit(4),
        cost_estimate=matmul_cost(rows, depth, count * 2 * BLOCK),
    )(normed, tail, vmem(w_gate), vmem(w_up), *after)


def gate_rows(own, moved, model):
    share, width = own.shape
    count = width // (2 * BLOCK)
    others = len(moved)

    def kernel(*refs):
        own, moved, out = refs[0], refs[1 : 1 + others], refs[-1]

        def total(here):
            value = own[:, here]
            for part in moved:
                value = value + part[:, here].astype(F32)
            return value

        tail = total(slice(count * 2 * BLOCK, count * 2 * BLOCK + HD))
        factor = lax.rsqrt((tail[:, 0:1] + tail[:, 1:2]) / model + EPSILON)
        for j in range(count):
            gate = total(slice(2 * j * BLOCK, (2 * j + 1) * BLOCK)) * factor
            up = total(slice((2 * j + 1) * BLOCK, (2 * j + 2) * BLOCK)) * factor
            out[:, j * BLOCK : (j + 1) * BLOCK] = (gate / (1.0 + jnp.exp(-gate)) * up).astype(BF16)

    return pl.pallas_call(
        kernel,
        name="gate",
        out_shape=jax.ShapeDtypeStruct((share, count * BLOCK), BF16),
        in_specs=[VMEM] * (1 + others),
        out_specs=VMEM,
        compiler_params=limit(4),
        cost_estimate=pl.CostEstimate(flops=WAIT, bytes_accessed=0, transcendentals=0),
    )(own, *moved)


def place_rows(chunks):
    sizes = [same.shape[1] for same, _ in chunks]
    rows = 2 * chunks[0][0].shape[0]

    def kernel(*refs):
        out, at = refs[-1], 0
        for k, size in enumerate(sizes):
            place_gathered(refs[2 * k], refs[2 * k + 1], out, slice(at, at + size))
            at += size

    return pl.pallas_call(
        kernel,
        name="place_rows",
        out_shape=jax.ShapeDtypeStruct((rows, sum(sizes)), BF16),
        in_specs=[VMEM] * (2 * len(sizes)),
        out_specs=VMEM,
        compiler_params=limit(4),
    )(*[x for pair in chunks for x in pair])


def finish(residual, terms):
    rows, columns = residual.shape
    half = columns // 2

    def kernel(residual, *refs):
        for first in (0, half):
            here = slice(first, first + half)
            total = add_terms(refs[:-1], here)
            refs[-1][:, here] = (residual[:, here].astype(F32) + total).astype(BF16)

    return pl.pallas_call(
        kernel,
        name="finish",
        out_shape=jax.ShapeDtypeStruct((rows, columns), BF16),
        in_specs=[VMEM] * (1 + len(terms)),
        out_specs=VMEM,
        compiler_params=limit(4),
    )(residual, *terms)


def local(
    incoming, queries, new_kv, cache, lengths, slot_of, w_out, norm_gain, w_gate, w_up, w_down
):
    ffn = lax.axis_size("ffn")
    att = lax.axis_size("att")
    requests = slot_of.shape[0]
    slots = cache.shape[0]
    model = w_out.shape[1]
    width = w_gate.shape[1]
    owned = requests // ffn

    whole = lambda x: (x, x.shape[0])
    queries, new_kv, token = load([whole(queries), whole(new_kv)], "load_new")
    qkv = jnp.concatenate([queries.reshape(slots, -1), new_kv.reshape(slots, -1)], axis=1)
    small = [whole(slot_of.reshape(1, requests)), whole(lengths.reshape(1, slots))]
    cache, slot_row, lengths, own, token = load(
        [whole(cache)] + small + [(incoming, owned)], "load_cache", [corner(qkv)]
    )
    own = own.reshape(owned, STEPS * model)
    same, other = gather_att(qkv, [token])
    attended = attend(lengths, slot_row, same, other, cache)
    w_out, token = load([whole(w_out)], "load_out", [corner(attended)])
    rows = order_rows(slot_row, *gather_att(attended, [token]))
    sums = reduce_ffn(*multiply(rows, w_out, "project"))

    residual, left, right = add_residual(own, sums)
    normed, tail = norm_rows(gather_ffn(residual, left, right), norm_gain.reshape(1, model))
    blocks, whole_of = width // BLOCK, sum(CHUNKS)
    edges = [blocks * sum(CHUNKS[:k]) // whole_of for k in range(len(CHUNKS) + 1)]
    pairs = []
    for k, (first, last) in enumerate(zip(edges[:-1], edges[1:])):
        after = [corner(keep)] if k == 1 else [corner(pairs[k - 2][1])] if k else []
        keep, send = widen(normed, tail, w_gate, w_up, first, last - first, after)
        pairs.append(add_parts(keep, exchange(send, "att", 1), att // 2, F32))
    moved = [
        [shift(part, "att", 2 * (d + 1)) for d, part in enumerate(away)] for _, *away in pairs
    ]
    chunks = [
        gather_att(gate_rows(pair[0], parts, model * att))
        for pair, parts in zip(pairs, moved)
    ]
    hidden = place_rows(chunks)
    out = finish(residual, reduce_ffn(*multiply(hidden, w_down, "narrow")))
    return jnp.swapaxes(out.reshape(STEPS, owned, model), 0, 1)


def solution(mesh):
    return jax.shard_map(
        local,
        mesh=mesh,
        in_specs=(
            P("parts", None, "att"),
            P(("parts", "att"), None, "ffn"),
            P(("parts", "att"), None, "ffn"),
            P(("parts", "att"), None, "ffn"),
            P(("parts", "att")),
            P("parts"),
            P("ffn", "att"),
            P("att"),
            P("att", "ffn"),
            P("att", "ffn"),
            P("ffn", "att"),
        ),
        out_specs=P(("parts", "ffn"), None, "att"),
        check_vma=False,
    )
```

profile of v0, /device:TPU:0, one launch (start us, length us, event | category | flops | bytes accessed | tf_op | source)
XLA Modules:
  0.0 92.3 jit_solution(6117073212576075905)
XLA Ops:
  0.0 1.6 %load_new.1 = (bf16[16,2,2048]{2,1,0:T(2,128)(2,1)S(1)}, bf16[16,2,512]{2,1,0:T(2,128)(2,1)S(1)}, f32[8,128]{1,0:T(8,128)}) custom-call(bf16[16,2,2048]{2,1,0:T(2,128)(2,1)} %refs_0_.3, bf16[16,2,512]{2,1,0:T(2,128)(2,1)} %refs_1_.1), custom_call_target="tpu_custom_call" | custom-call | bytes 327680 | tf_op jit(solution)/shard_map/load_new/pallas_call | solution.py:160
  1.7 3.0 %collective-permute-start = (bf16[16,5120]{1,0:T(8,128)(2,1)S(1)}, bf16[16,5120]{1,0:T(8,128)(2,1)S(1)}, u32[]{:S(2)}, u32[]{:S(2)}) collective-permute-start(bf16[16,5120]{1,0:T(8,128)(2,1)S(1)} %constant_dynamic-update-slice_fusion.refs_0_), channel_id=1, source_target_pairs={{0,8},{4,12},{8,0},{12,4},{1,9},{5,13},{9,1},{13,5},{2,10},{6,14},... | collective-permute-start | bytes 491528 | tf_op jit(solution)/shard_map/ppermute | solution.py:33
  4.8 4.4 %load_cache.1 = (bf16[16,640,512]{2,1,0:T(8,128)(2,1)S(1)}, s32[1,64]{1,0:T(1,128)S(1)}, s32[1,16]{1,0:T(1,128)S(1)}, bf16[16,2,2048]{2,1,0:T(2,128)(2,1)S(1)}, f32[8,128]{1,0:T(8,128)S(1)}) custom-call(bf16[16,640,512]{2,1,0:T(8,128)(2,1)} %refs_0_.4, s32[1,64]{1,0:T(1,128)} %bitcast.28, s32[1,16]{1,0:T(1,128)} %bitcast.29, bf16[64,2,2048]{2,1,0:T(2,128)(2,1)} %refs_3_.1, ...), custom_call_target="tpu_custom_call" | custom-call | bytes 21234304 | tf_op jit(solution)/shard_map/load_cache/pallas_call | solution.py:160
  9.3 1.6 %collective-permute-done.1.other = bf16[32,5120]{1,0:T(8,128)(2,1)S(1)} collective-permute-done((bf16[32,5120]{1,0:T(8,128)(2,1)S(1)}, bf16[32,5120]{1,0:T(8,128)(2,1)S(1)}, u32[]{:S(2)}, u32[]{:S(2)}) %collective-permute-start.1) | collective-permute-done | bytes 327712 | tf_op jit(solution)/shard_map/ppermute | solution.py:37
  11.0 2.9 %attend.1.refs_0_ = bf16[32,2048]{1,0:T(8,128)(2,1)S(1)} custom-call(s32[1,16]{1,0:T(1,128)S(1)} %get-tuple-element.46.lengths, s32[1,64]{1,0:T(1,128)S(1)} %get-tuple-element.45.slot_row, bf16[32,5120]{1,0:T(8,128)(2,1)S(1)} %join.5.same, bf16[32,5120]{1,0:T(8,128)(2,1)S(1)} %collective-permute-done.1.other, bf16[16,640,512]{2,1,0:T(8,128)(2,1)S(1)} %get-tuple-element.49.cache), custom_call_target="tpu_custom_call" | custom-call | flops 671088640 | bytes 10485760 | tf_op jit(solution)/shard_map/attend/pallas_call | solution.py:242
  13.9 1.5 %collective-permute-start.2 = (bf16[32,2048]{1,0:T(8,128)(2,1)S(1)}, bf16[32,2048]{1,0:T(8,128)(2,1)S(1)}, u32[]{:S(2)}, u32[]{:S(2)}) collective-permute-start(bf16[32,2048]{1,0:T(8,128)(2,1)S(1)} %attend.1.refs_0_), channel_id=1, source_target_pairs={{0,8},{4,12},{8,0},{12,4},{1,9},{5,13},{9,1},{13,5},{2,10},{6,14},... | collective-permute-start | bytes 393224 | tf_op jit(solution)/shard_map/ppermute | solution.py:33
  15.4 3.6 %load_out.1 = (bf16[2048,2048]{1,0:T(8,128)(2,1)S(1)}, f32[8,128]{1,0:T(8,128)S(1)}) custom-call(bf16[2048,2048]{1,0:T(8,128)(2,1)} %refs_0_.5, bf16[8,128]{1,0:T(8,128)(2,1)S(1)} %slice.17.refs_1_), custom_call_target="tpu_custom_call" | custom-call | bytes 16777216 | tf_op jit(solution)/shard_map/load_out/pallas_call | solution.py:160
  19.6 1.5 %collective-permute-done.3.other = bf16[64,2048]{1,0:T(8,128)(2,1)S(1)} collective-permute-done((bf16[64,2048]{1,0:T(8,128)(2,1)S(1)}, bf16[64,2048]{1,0:T(8,128)(2,1)S(1)}, u32[]{:S(2)}, u32[]{:S(2)}) %collective-permute-start.3) | collective-permute-done | bytes 262176 | tf_op jit(solution)/shard_map/ppermute | solution.py:37
  22.8 1.6 %collective-permute-start.6 = (bf16[32,1024]{1,0:T(8,128)(2,1)S(1)}, bf16[32,1024]{1,0:T(8,128)(2,1)S(1)}, u32[]{:S(2)}, u32[]{:S(2)}) collective-permute-start(bf16[32,1024]{1,0:T(8,128)(2,1)S(1)} %get-tuple-element.56), channel_id=1, source_target_pairs={{0,1},{1,0},{2,3},{3,2},{4,5},{5,4},{6,7},{7,6},{8,9},{9,8},{10,11... | collective-permute-start | bytes 196616 | tf_op jit(solution)/shard_map/ppermute | solution.py:37
  24.9 2.6 %collective-permute-start.4 = (bf16[32,1024]{1,0:T(8,128)(2,1)S(1)}, bf16[32,1024]{1,0:T(8,128)(2,1)S(1)}, u32[]{:S(2)}, u32[]{:S(2)}) collective-permute-start(bf16[32,1024]{1,0:T(8,128)(2,1)S(1)} %get-tuple-element.53), channel_id=1, source_target_pairs={{0,2},{1,3},{2,0},{3,1},{4,6},{5,7},{6,4},{7,5},{8,10},{9,11},{10,... | collective-permute-start | bytes 196616 | tf_op jit(solution)/shard_map/ppermute | solution.py:37
  27.5 1.3 %collective-permute-start.5 = (bf16[32,1024]{1,0:T(8,128)(2,1)S(1)}, bf16[32,1024]{1,0:T(8,128)(2,1)S(1)}, u32[]{:S(2)}, u32[]{:S(2)}) collective-permute-start(bf16[32,1024]{1,0:T(8,128)(2,1)S(1)} %get-tuple-element.54), channel_id=1, source_target_pairs={{0,3},{1,2},{2,1},{3,0},{4,7},{5,6},{6,5},{7,4},{8,11},{9,10},{10,... | collective-permute-start | bytes 196616 | tf_op jit(solution)/shard_map/ppermute | solution.py:37
  28.9 1.8 %collective-permute-start.7 = (bf16[32,1024]{1,0:T(8,128)(2,1)S(1)}, bf16[32,1024]{1,0:T(8,128)(2,1)S(1)}, u32[]{:S(2)}, u32[]{:S(2)}) collective-permute-start(bf16[32,1024]{1,0:T(8,128)(2,1)S(1)} %add_parts.5), channel_id=1, source_target_pairs={{0,2},{1,3},{2,0},{3,1},{4,6},{5,7},{6,4},{7,5},{8,10},{9,11},{10,... | collective-permute-start | bytes 196616 | tf_op jit(solution)/shard_map/ppermute | solution.py:37
  31.2 4.4 %collective-permute-done.5.refs_2_ = bf16[32,1024]{1,0:T(8,128)(2,1)S(1)} collective-permute-done((bf16[32,1024]{1,0:T(8,128)(2,1)S(1)}, bf16[32,1024]{1,0:T(8,128)(2,1)S(1)}, u32[]{:S(2)}, u32[]{:S(2)}) %collective-permute-start.5) | collective-permute-done | bytes 65568 | tf_op jit(solution)/shard_map/ppermute | solution.py:37
  35.6 2.0 %collective-permute-done.7.refs_3_ = bf16[32,1024]{1,0:T(8,128)(2,1)S(1)} collective-permute-done((bf16[32,1024]{1,0:T(8,128)(2,1)S(1)}, bf16[32,1024]{1,0:T(8,128)(2,1)S(1)}, u32[]{:S(2)}, u32[]{:S(2)}) %collective-permute-start.7) | collective-permute-done | bytes 65568 | tf_op jit(solution)/shard_map/ppermute | solution.py:37
  38.6 2.2 %collective-permute-start.9 = (bf16[32,2048]{1,0:T(8,128)(2,1)S(1)}, bf16[32,2048]{1,0:T(8,128)(2,1)S(1)}, u32[]{:S(2)}, u32[]{:S(2)}) collective-permute-start(bf16[32,2048]{1,0:T(8,128)(2,1)S(1)} %get-tuple-element.58.refs_5_.residual), channel_id=1, source_target_pairs={{0,1},{1,0},{2,3},{3,2},{4,5},{5,4},{6,7},{7,6},{8,9},{9,8},{10,11... | collective-permute-start | bytes 393224 | tf_op jit(solution)/shard_map/ppermute | solution.py:37
  40.8 2.3 %collective-permute-start.12 = (bf16[32,1024]{1,0:T(8,128)(2,1)S(1)}, bf16[32,1024]{1,0:T(8,128)(2,1)S(1)}, u32[]{:S(2)}, u32[]{:S(2)}) collective-permute-start(bf16[32,1024]{1,0:T(8,128)(2,1)S(1)} %get-tuple-element.60), channel_id=1, source_target_pairs={{0,3},{1,2},{2,1},{3,0},{4,7},{5,6},{6,5},{7,4},{8,11},{9,10},{10,... | collective-permute-start | bytes 196616 | tf_op jit(solution)/shard_map/ppermute | solution.py:37
  43.1 2.0 %collective-permute-done.10.refs_2_ = bf16[32,1024]{1,0:T(8,128)(2,1)S(1)} collective-permute-done((bf16[32,1024]{1,0:T(8,128)(2,1)S(1)}, bf16[32,1024]{1,0:T(8,128)(2,1)S(1)}, u32[]{:S(2)}, u32[]{:S(2)}) %collective-permute-start.10) | collective-permute-done | bytes 65568 | tf_op jit(solution)/shard_map/ppermute | solution.py:37
  45.1 2.1 %collective-permute-done.13.refs_4_ = bf16[32,1024]{1,0:T(8,128)(2,1)S(1)} collective-permute-done((bf16[32,1024]{1,0:T(8,128)(2,1)S(1)}, bf16[32,1024]{1,0:T(8,128)(2,1)S(1)}, u32[]{:S(2)}, u32[]{:S(2)}) %collective-permute-start.13) | collective-permute-done | bytes 65568 | tf_op jit(solution)/shard_map/ppermute | solution.py:37
  49.7 1.3 %widen.3 = (bf16[64,2176]{1,0:T(8,128)(2,1)S(1)}, bf16[64,2176]{1,0:T(8,128)(2,1)S(1)}) custom-call(bf16[128,2048]{1,0:T(8,128)(2,1)S(1)} %get-tuple-element.61.normed, bf16[128,128]{1,0:T(8,128)(2,1)S(1)} %get-tuple-element.62.tail, bf16[2048,3584]{1,0:T(8,128)(2,1)S(1)} %bitcast.14, bf16[2048,3584]{1,0:T(8,128)(2,1)S(1)} %bitcast.16), custom_call_target="tpu_custom_call" | custom-call | flops 1073741824 | bytes 9437184 | tf_op jit(solution)/shard_map/widen/pallas_call | solution.py:454
  51.1 1.9 %widen.4 = (bf16[64,3200]{1,0:T(8,128)(2,1)S(1)}, bf16[64,3200]{1,0:T(8,128)(2,1)S(1)}) custom-call(bf16[128,2048]{1,0:T(8,128)(2,1)S(1)} %get-tuple-element.61.normed, bf16[128,128]{1,0:T(8,128)(2,1)S(1)} %get-tuple-element.62.tail, bf16[2048,3584]{1,0:T(8,128)(2,1)S(1)} %bitcast.14, bf16[2048,3584]{1,0:T(8,128)(2,1)S(1)} %bitcast.16, ...), custom_call_target="tpu_custom_call" | custom-call | flops 1610612736 | bytes 13893632 | tf_op jit(solution)/shard_map/widen/pallas_call | solution.py:454
  53.7 1.5 %collective-permute-start.15 = (bf16[32,2176]{1,0:T(8,128)(2,1)S(1)}, bf16[32,2176]{1,0:T(8,128)(2,1)S(1)}, u32[]{:S(2)}, u32[]{:S(2)}) collective-permute-start(bf16[32,2176]{1,0:T(8,128)(2,1)S(1)} %get-tuple-element.66), channel_id=1, source_target_pairs={{0,8},{4,12},{8,0},{12,4},{1,9},{5,13},{9,1},{13,5},{2,10},{6,14},... | collective-permute-start | bytes 417800 | tf_op jit(solution)/shard_map/ppermute | solution.py:33
  57.4 2.0 %collective-permute-done.15.refs_1_ = bf16[32,2176]{1,0:T(8,128)(2,1)S(1)} collective-permute-done((bf16[32,2176]{1,0:T(8,128)(2,1)S(1)}, bf16[32,2176]{1,0:T(8,128)(2,1)S(1)}, u32[]{:S(2)}, u32[]{:S(2)}) %collective-permute-start.15) | collective-permute-done | bytes 139296 | tf_op jit(solution)/shard_map/ppermute | solution.py:33
  59.6 1.8 %collective-permute-start.16 = (bf16[32,1024]{1,0:T(8,128)(2,1)S(1)}, bf16[32,1024]{1,0:T(8,128)(2,1)S(1)}, u32[]{:S(2)}, u32[]{:S(2)}) collective-permute-start(bf16[32,1024]{1,0:T(8,128)(2,1)S(1)} %gate.7.refs_0_), channel_id=1, source_target_pairs={{0,8},{4,12},{8,0},{12,4},{1,9},{5,13},{9,1},{13,5},{2,10},{6,14},... | collective-permute-start | bytes 196616 | tf_op jit(solution)/shard_map/ppermute | solution.py:33
  61.8 2.9 %collective-permute-done.19.refs_1_ = bf16[32,3200]{1,0:T(8,128)(2,1)S(1)} collective-permute-done((bf16[32,3200]{1,0:T(8,128)(2,1)S(1)}, bf16[32,3200]{1,0:T(8,128)(2,1)S(1)}, u32[]{:S(2)}, u32[]{:S(2)}) %collective-permute-start.19) | collective-permute-done | bytes 204832 | tf_op jit(solution)/shard_map/ppermute | solution.py:33
  65.8 3.3 %collective-permute-done.23.refs_1_ = bf16[32,2176]{1,0:T(8,128)(2,1)S(1)} collective-permute-done((bf16[32,2176]{1,0:T(8,128)(2,1)S(1)}, bf16[32,2176]{1,0:T(8,128)(2,1)S(1)}, u32[]{:S(2)}, u32[]{:S(2)}) %collective-permute-start.23) | collective-permute-done | bytes 139296 | tf_op jit(solution)/shard_map/ppermute | solution.py:33
  71.5 2.1 %collective-permute-done.24.refs_1_ = bf16[32,1024]{1,0:T(8,128)(2,1)S(1)} collective-permute-done((bf16[32,1024]{1,0:T(8,128)(2,1)S(1)}, bf16[32,1024]{1,0:T(8,128)(2,1)S(1)}, u32[]{:S(2)}, u32[]{:S(2)}) %collective-permute-start.24) | collective-permute-done | bytes 65568 | tf_op jit(solution)/shard_map/ppermute | solution.py:33
  75.2 2.1 %narrow.1 = (f32[32,2048]{1,0:T(8,128)S(1)}, bf16[32,2048]{1,0:T(8,128)(2,1)S(1)}, f32[32,1024]{1,0:T(8,128)S(1)}, bf16[32,1024]{1,0:T(8,128)(2,1)S(1)}, bf16[32...) custom-call(bf16[128,3584]{1,0:T(8,128)(2,1)S(1)} %place_rows.1.rows, bf16[3584,2048]{1,0:T(8,128)(2,1)S(1)} %bitcast.18), custom_call_target="tpu_custom_call" | custom-call | flops 1879048192 | bytes 16121856 | tf_op jit(solution)/shard_map/narrow/pallas_call | solution.py:334
  77.5 1.8 %collective-permute-start.30 = (bf16[32,2048]{1,0:T(8,128)(2,1)S(1)}, bf16[32,2048]{1,0:T(8,128)(2,1)S(1)}, u32[]{:S(2)}, u32[]{:S(2)}) collective-permute-start(bf16[32,2048]{1,0:T(8,128)(2,1)S(1)} %get-tuple-element.80), channel_id=1, source_target_pairs={{0,1},{1,0},{2,3},{3,2},{4,5},{5,4},{6,7},{7,6},{8,9},{9,8},{10,11... | collective-permute-start | bytes 393224 | tf_op jit(solution)/shard_map/ppermute | solution.py:37
  80.4 1.5 %collective-permute-start.27 = (bf16[32,1024]{1,0:T(8,128)(2,1)S(1)}, bf16[32,1024]{1,0:T(8,128)(2,1)S(1)}, u32[]{:S(2)}, u32[]{:S(2)}) collective-permute-start(bf16[32,1024]{1,0:T(8,128)(2,1)S(1)} %get-tuple-element.77), channel_id=1, source_target_pairs={{0,3},{1,2},{2,1},{3,0},{4,7},{5,6},{6,5},{7,4},{8,11},{9,10},{10,... | collective-permute-start | bytes 196616 | tf_op jit(solution)/shard_map/ppermute | solution.py:37
  82.3 1.7 %collective-permute-start.29 = (bf16[32,1024]{1,0:T(8,128)(2,1)S(1)}, bf16[32,1024]{1,0:T(8,128)(2,1)S(1)}, u32[]{:S(2)}, u32[]{:S(2)}) collective-permute-start(bf16[32,1024]{1,0:T(8,128)(2,1)S(1)} %add_parts.9), channel_id=1, source_target_pairs={{0,2},{1,3},{2,0},{3,1},{4,6},{5,7},{6,4},{7,5},{8,10},{9,11},{10,... | collective-permute-start | bytes 196616 | tf_op jit(solution)/shard_map/ppermute | solution.py:37
  83.9 5.5 %collective-permute-done.26.refs_1_ = bf16[32,1024]{1,0:T(8,128)(2,1)S(1)} collective-permute-done((bf16[32,1024]{1,0:T(8,128)(2,1)S(1)}, bf16[32,1024]{1,0:T(8,128)(2,1)S(1)}, u32[]{:S(2)}, u32[]{:S(2)}) %collective-permute-start.26) | collective-permute-done | bytes 65568 | tf_op jit(solution)/shard_map/ppermute | solution.py:37
  89.4 2.0 %collective-permute-done.29.refs_3_ = bf16[32,1024]{1,0:T(8,128)(2,1)S(1)} collective-permute-done((bf16[32,1024]{1,0:T(8,128)(2,1)S(1)}, bf16[32,1024]{1,0:T(8,128)(2,1)S(1)}, u32[]{:S(2)}, u32[]{:S(2)}) %collective-permute-start.29) | collective-permute-done | bytes 65568 | tf_op jit(solution)/shard_map/ppermute | solution.py:37
  (96 shorter events, 17.9 us)
Async XLA Ops:
  1.7 7.5 %collective-permute-start = (bf16[16,5120]{1,0:T(8,128)(2,1)S(1)}, bf16[16,5120]{1,0:T(8,128)(2,1)S(1)}, u32[]{:S(2)}, u32[]{:S(2)}) collective-permute-start(bf16[16,5120]{1,0:T(8,128)(2,1)S(1)} %constant_dynamic-update-slice_fusion.refs_0_), channel_id=1, source_target_pairs={{0,8},{4,12},{8,0},{12,4},{1,9},{5,13},{9,1},{13,5},{2,10},{6,14},... | collective-permute-start | bytes 491528 | tf_op jit(solution)/shard_map/ppermute | solution.py:33
  4.8 44.9 %slice-start.5 = ((s8[14680064]{0:T(1024)(128)(4,1)}), s8[4194304]{0:T(1024)(128)(4,1)S(1)}, s32[]{:S(2)}) async-start(s8[14680064]{0:T(1024)(128)(4,1)} %bitcast.15), calls=%async_computation.5 | async-start | bytes 8388608
  9.3 1.7 %collective-permute-start.1 = (bf16[32,5120]{1,0:T(8,128)(2,1)S(1)}, bf16[32,5120]{1,0:T(8,128)(2,1)S(1)}, u32[]{:S(2)}, u32[]{:S(2)}) collective-permute-start(bf16[32,5120]{1,0:T(8,128)(2,1)S(1)} %join.5.same), channel_id=1, source_target_pairs={{0,4},{4,0},{8,12},{12,8},{1,5},{5,1},{9,13},{13,9},{2,6},{6,2},{1... | collective-permute-start | bytes 983048 | tf_op jit(solution)/shard_map/ppermute | solution.py:37
  13.9 5.6 %collective-permute-start.2 = (bf16[32,2048]{1,0:T(8,128)(2,1)S(1)}, bf16[32,2048]{1,0:T(8,128)(2,1)S(1)}, u32[]{:S(2)}, u32[]{:S(2)}) collective-permute-start(bf16[32,2048]{1,0:T(8,128)(2,1)S(1)} %attend.1.refs_0_), channel_id=1, source_target_pairs={{0,8},{4,12},{8,0},{12,4},{1,9},{5,13},{9,1},{13,5},{2,10},{6,14},... | collective-permute-start | bytes 393224 | tf_op jit(solution)/shard_map/ppermute | solution.py:33
  19.5 1.6 %collective-permute-start.3 = (bf16[64,2048]{1,0:T(8,128)(2,1)S(1)}, bf16[64,2048]{1,0:T(8,128)(2,1)S(1)}, u32[]{:S(2)}, u32[]{:S(2)}) collective-permute-start(bf16[64,2048]{1,0:T(8,128)(2,1)S(1)} %join.6.same), channel_id=1, source_target_pairs={{0,4},{4,0},{8,12},{12,8},{1,5},{5,1},{9,13},{13,9},{2,6},{6,2},{1... | collective-permute-start | bytes 786440 | tf_op jit(solution)/shard_map/ppermute | solution.py:37
  22.8 6.0 %collective-permute-start.6 = (bf16[32,1024]{1,0:T(8,128)(2,1)S(1)}, bf16[32,1024]{1,0:T(8,128)(2,1)S(1)}, u32[]{:S(2)}, u32[]{:S(2)}) collective-permute-start(bf16[32,1024]{1,0:T(8,128)(2,1)S(1)} %get-tuple-element.56), channel_id=1, source_target_pairs={{0,1},{1,0},{2,3},{3,2},{4,5},{5,4},{6,7},{7,6},{8,9},{9,8},{10,11... | collective-permute-start | bytes 196616 | tf_op jit(solution)/shard_map/ppermute | solution.py:37
  24.5 11.1 %collective-permute-start.8 = (bf16[32,2048]{1,0:T(8,128)(2,1)S(1)}, bf16[32,2048]{1,0:T(8,128)(2,1)S(1)}, u32[]{:S(2)}, u32[]{:S(2)}) collective-permute-start(bf16[32,2048]{1,0:T(8,128)(2,1)S(1)} %get-tuple-element.57), channel_id=1, source_target_pairs={{0,1},{1,0},{2,3},{3,2},{4,5},{5,4},{6,7},{7,6},{8,9},{9,8},{10,11... | collective-permute-start | bytes 393224 | tf_op jit(solution)/shard_map/ppermute | solution.py:37
  24.9 6.3 %collective-permute-start.4 = (bf16[32,1024]{1,0:T(8,128)(2,1)S(1)}, bf16[32,1024]{1,0:T(8,128)(2,1)S(1)}, u32[]{:S(2)}, u32[]{:S(2)}) collective-permute-start(bf16[32,1024]{1,0:T(8,128)(2,1)S(1)} %get-tuple-element.53), channel_id=1, source_target_pairs={{0,2},{1,3},{2,0},{3,1},{4,6},{5,7},{6,4},{7,5},{8,10},{9,11},{10,... | collective-permute-start | bytes 196616 | tf_op jit(solution)/shard_map/ppermute | solution.py:37
  27.5 8.1 %collective-permute-start.5 = (bf16[32,1024]{1,0:T(8,128)(2,1)S(1)}, bf16[32,1024]{1,0:T(8,128)(2,1)S(1)}, u32[]{:S(2)}, u32[]{:S(2)}) collective-permute-start(bf16[32,1024]{1,0:T(8,128)(2,1)S(1)} %get-tuple-element.54), channel_id=1, source_target_pairs={{0,3},{1,2},{2,1},{3,0},{4,7},{5,6},{6,5},{7,4},{8,11},{9,10},{10,... | collective-permute-start | bytes 196616 | tf_op jit(solution)/shard_map/ppermute | solution.py:37
  28.9 8.7 %collective-permute-start.7 = (bf16[32,1024]{1,0:T(8,128)(2,1)S(1)}, bf16[32,1024]{1,0:T(8,128)(2,1)S(1)}, u32[]{:S(2)}, u32[]{:S(2)}) collective-permute-start(bf16[32,1024]{1,0:T(8,128)(2,1)S(1)} %add_parts.5), channel_id=1, source_target_pairs={{0,2},{1,3},{2,0},{3,1},{4,6},{5,7},{6,4},{7,5},{8,10},{9,11},{10,... | collective-permute-start | bytes 196616 | tf_op jit(solution)/shard_map/ppermute | solution.py:37
  37.7 7.4 %collective-permute-start.10 = (bf16[32,1024]{1,0:T(8,128)(2,1)S(1)}, bf16[32,1024]{1,0:T(8,128)(2,1)S(1)}, u32[]{:S(2)}, u32[]{:S(2)}) collective-permute-start(bf16[32,1024]{1,0:T(8,128)(2,1)S(1)} %get-tuple-element.59), channel_id=1, source_target_pairs={{0,2},{1,3},{2,0},{3,1},{4,6},{5,7},{6,4},{7,5},{8,10},{9,11},{10,... | collective-permute-start | bytes 196616 | tf_op jit(solution)/shard_map/ppermute | solution.py:37
  38.6 9.8 %collective-permute-start.9 = (bf16[32,2048]{1,0:T(8,128)(2,1)S(1)}, bf16[32,2048]{1,0:T(8,128)(2,1)S(1)}, u32[]{:S(2)}, u32[]{:S(2)}) collective-permute-start(bf16[32,2048]{1,0:T(8,128)(2,1)S(1)} %get-tuple-element.58.refs_5_.residual), channel_id=1, source_target_pairs={{0,1},{1,0},{2,3},{3,2},{4,5},{5,4},{6,7},{7,6},{8,9},{9,8},{10,11... | collective-permute-start | bytes 393224 | tf_op jit(solution)/shard_map/ppermute | solution.py:37
  40.7 6.4 %collective-permute-start.13 = (bf16[32,1024]{1,0:T(8,128)(2,1)S(1)}, bf16[32,1024]{1,0:T(8,128)(2,1)S(1)}, u32[]{:S(2)}, u32[]{:S(2)}) collective-permute-start(bf16[32,1024]{1,0:T(8,128)(2,1)S(1)} %get-tuple-element.60), channel_id=1, source_target_pairs={{0,2},{1,3},{2,0},{3,1},{4,6},{5,7},{6,4},{7,5},{8,10},{9,11},{10,... | collective-permute-start | bytes 196616 | tf_op jit(solution)/shard_map/ppermute | solution.py:37
  40.8 7.5 %collective-permute-start.12 = (bf16[32,1024]{1,0:T(8,128)(2,1)S(1)}, bf16[32,1024]{1,0:T(8,128)(2,1)S(1)}, u32[]{:S(2)}, u32[]{:S(2)}) collective-permute-start(bf16[32,1024]{1,0:T(8,128)(2,1)S(1)} %get-tuple-element.60), channel_id=1, source_target_pairs={{0,3},{1,2},{2,1},{3,0},{4,7},{5,6},{6,5},{7,4},{8,11},{9,10},{10,... | collective-permute-start | bytes 196616 | tf_op jit(solution)/shard_map/ppermute | solution.py:37
  45.1 4.3 %collective-permute-start.11 = (bf16[32,1024]{1,0:T(8,128)(2,1)S(1)}, bf16[32,1024]{1,0:T(8,128)(2,1)S(1)}, u32[]{:S(2)}, u32[]{:S(2)}) collective-permute-start(bf16[32,1024]{1,0:T(8,128)(2,1)S(1)} %collective-permute-done.10.refs_2_), channel_id=1, source_target_pairs={{0,1},{1,0},{2,3},{3,2},{4,5},{5,4},{6,7},{7,6},{8,9},{9,8},{10,11... | collective-permute-start | bytes 196616 | tf_op jit(solution)/shard_map/ppermute | solution.py:37
  51.1 2.6 %collective-permute-start.14 = (bf16[64,2176]{1,0:T(8,128)(2,1)S(1)}, bf16[64,2176]{1,0:T(8,128)(2,1)S(1)}, u32[]{:S(2)}, u32[]{:S(2)}) collective-permute-start(bf16[64,2176]{1,0:T(8,128)(2,1)S(1)} %get-tuple-element.64), channel_id=1, source_target_pairs={{0,4},{4,0},{8,12},{12,8},{1,5},{5,1},{9,13},{13,9},{2,6},{6,2},{1... | collective-permute-start | bytes 835592 | tf_op jit(solution)/shard_map/ppermute | solution.py:37
  53.1 3.6 %collective-permute-start.18 = (bf16[64,3200]{1,0:T(8,128)(2,1)S(1)}, bf16[64,3200]{1,0:T(8,128)(2,1)S(1)}, u32[]{:S(2)}, u32[]{:S(2)}) collective-permute-start(bf16[64,3200]{1,0:T(8,128)(2,1)S(1)} %get-tuple-element.68), channel_id=1, source_target_pairs={{0,4},{4,0},{8,12},{12,8},{1,5},{5,1},{9,13},{13,9},{2,6},{6,2},{1... | collective-permute-start | bytes 1228808 | tf_op jit(solution)/shard_map/ppermute | solution.py:37
  53.7 5.7 %collective-permute-start.15 = (bf16[32,2176]{1,0:T(8,128)(2,1)S(1)}, bf16[32,2176]{1,0:T(8,128)(2,1)S(1)}, u32[]{:S(2)}, u32[]{:S(2)}) collective-permute-start(bf16[32,2176]{1,0:T(8,128)(2,1)S(1)} %get-tuple-element.66), channel_id=1, source_target_pairs={{0,8},{4,12},{8,0},{12,4},{1,9},{5,13},{9,1},{13,5},{2,10},{6,14},... | collective-permute-start | bytes 417800 | tf_op jit(solution)/shard_map/ppermute | solution.py:33
  56.5 4.8 %collective-permute-start.22 = (bf16[64,2176]{1,0:T(8,128)(2,1)S(1)}, bf16[64,2176]{1,0:T(8,128)(2,1)S(1)}, u32[]{:S(2)}, u32[]{:S(2)}) collective-permute-start(bf16[64,2176]{1,0:T(8,128)(2,1)S(1)} %get-tuple-element.72), channel_id=1, source_target_pairs={{0,4},{4,0},{8,12},{12,8},{1,5},{5,1},{9,13},{13,9},{2,6},{6,2},{1... | collective-permute-start | bytes 835592 | tf_op jit(solution)/shard_map/ppermute | solution.py:37
  56.7 7.9 %collective-permute-start.19 = (bf16[32,3200]{1,0:T(8,128)(2,1)S(1)}, bf16[32,3200]{1,0:T(8,128)(2,1)S(1)}, u32[]{:S(2)}, u32[]{:S(2)}) collective-permute-start(bf16[32,3200]{1,0:T(8,128)(2,1)S(1)} %get-tuple-element.70), channel_id=1, source_target_pairs={{0,8},{4,12},{8,0},{12,4},{1,9},{5,13},{9,1},{13,5},{2,10},{6,14},... | collective-permute-start | bytes 614408 | tf_op jit(solution)/shard_map/ppermute | solution.py:33
  59.6 11.3 %collective-permute-start.16 = (bf16[32,1024]{1,0:T(8,128)(2,1)S(1)}, bf16[32,1024]{1,0:T(8,128)(2,1)S(1)}, u32[]{:S(2)}, u32[]{:S(2)}) collective-permute-start(bf16[32,1024]{1,0:T(8,128)(2,1)S(1)} %gate.7.refs_0_), channel_id=1, source_target_pairs={{0,8},{4,12},{8,0},{12,4},{1,9},{5,13},{9,1},{13,5},{2,10},{6,14},... | collective-permute-start | bytes 196616 | tf_op jit(solution)/shard_map/ppermute | solution.py:33
  61.4 7.7 %collective-permute-start.23 = (bf16[32,2176]{1,0:T(8,128)(2,1)S(1)}, bf16[32,2176]{1,0:T(8,128)(2,1)S(1)}, u32[]{:S(2)}, u32[]{:S(2)}) collective-permute-start(bf16[32,2176]{1,0:T(8,128)(2,1)S(1)} %get-tuple-element.74), channel_id=1, source_target_pairs={{0,8},{4,12},{8,0},{12,4},{1,9},{5,13},{9,1},{13,5},{2,10},{6,14},... | collective-permute-start | bytes 417800 | tf_op jit(solution)/shard_map/ppermute | solution.py:33
  64.9 5.9 %collective-permute-start.20 = (bf16[32,1536]{1,0:T(8,128)(2,1)S(1)}, bf16[32,1536]{1,0:T(8,128)(2,1)S(1)}, u32[]{:S(2)}, u32[]{:S(2)}) collective-permute-start(bf16[32,1536]{1,0:T(8,128)(2,1)S(1)} %gate.9.refs_0_), channel_id=1, source_target_pairs={{0,8},{4,12},{8,0},{12,4},{1,9},{5,13},{9,1},{13,5},{2,10},{6,14},... | collective-permute-start | bytes 294920 | tf_op jit(solution)/shard_map/ppermute | solution.py:33
  69.3 4.3 %collective-permute-start.24 = (bf16[32,1024]{1,0:T(8,128)(2,1)S(1)}, bf16[32,1024]{1,0:T(8,128)(2,1)S(1)}, u32[]{:S(2)}, u32[]{:S(2)}) collective-permute-start(bf16[32,1024]{1,0:T(8,128)(2,1)S(1)} %gate.11.refs_0_), channel_id=1, source_target_pairs={{0,8},{4,12},{8,0},{12,4},{1,9},{5,13},{9,1},{13,5},{2,10},{6,14},... | collective-permute-start | bytes 196616 | tf_op jit(solution)/shard_map/ppermute | solution.py:33
  70.8 4.2 %collective-permute-start.21 = (bf16[64,1536]{1,0:T(8,128)(2,1)S(1)}, bf16[64,1536]{1,0:T(8,128)(2,1)S(1)}, u32[]{:S(2)}, u32[]{:S(2)}) collective-permute-start(bf16[64,1536]{1,0:T(8,128)(2,1)S(1)} %join.8.refs_2_), channel_id=1, source_target_pairs={{0,4},{4,0},{8,12},{12,8},{1,5},{5,1},{9,13},{13,9},{2,6},{6,2},{1... | collective-permute-start | bytes 589832 | tf_op jit(solution)/shard_map/ppermute | solution.py:37
  70.9 2.8 %collective-permute-start.17 = (bf16[64,1024]{1,0:T(8,128)(2,1)S(1)}, bf16[64,1024]{1,0:T(8,128)(2,1)S(1)}, u32[]{:S(2)}, u32[]{:S(2)}) collective-permute-start(bf16[64,1024]{1,0:T(8,128)(2,1)S(1)} %join.7.refs_0_), channel_id=1, source_target_pairs={{0,4},{4,0},{8,12},{12,8},{1,5},{5,1},{9,13},{13,9},{2,6},{6,2},{1... | collective-permute-start | bytes 393224 | tf_op jit(solution)/shard_map/ppermute | solution.py:37
  73.6 1.4 %collective-permute-start.25 = (bf16[64,1024]{1,0:T(8,128)(2,1)S(1)}, bf16[64,1024]{1,0:T(8,128)(2,1)S(1)}, u32[]{:S(2)}, u32[]{:S(2)}) collective-permute-start(bf16[64,1024]{1,0:T(8,128)(2,1)S(1)} %join.9.refs_4_), channel_id=1, source_target_pairs={{0,4},{4,0},{8,12},{12,8},{1,5},{5,1},{9,13},{13,9},{2,6},{6,2},{1... | collective-permute-start | bytes 393224 | tf_op jit(solution)/shard_map/ppermute | solution.py:37
  77.2 5.0 %collective-permute-start.28 = (bf16[32,1024]{1,0:T(8,128)(2,1)S(1)}, bf16[32,1024]{1,0:T(8,128)(2,1)S(1)}, u32[]{:S(2)}, u32[]{:S(2)}) collective-permute-start(bf16[32,1024]{1,0:T(8,128)(2,1)S(1)} %get-tuple-element.79), channel_id=1, source_target_pairs={{0,1},{1,0},{2,3},{3,2},{4,5},{5,4},{6,7},{7,6},{8,9},{9,8},{10,11... | collective-permute-start | bytes 196616 | tf_op jit(solution)/shard_map/ppermute | solution.py:37
  77.5 13.9 %collective-permute-start.30 = (bf16[32,2048]{1,0:T(8,128)(2,1)S(1)}, bf16[32,2048]{1,0:T(8,128)(2,1)S(1)}, u32[]{:S(2)}, u32[]{:S(2)}) collective-permute-start(bf16[32,2048]{1,0:T(8,128)(2,1)S(1)} %get-tuple-element.80), channel_id=1, source_target_pairs={{0,1},{1,0},{2,3},{3,2},{4,5},{5,4},{6,7},{7,6},{8,9},{9,8},{10,11... | collective-permute-start | bytes 393224 | tf_op jit(solution)/shard_map/ppermute | solution.py:37
  79.3 10.1 %collective-permute-start.26 = (bf16[32,1024]{1,0:T(8,128)(2,1)S(1)}, bf16[32,1024]{1,0:T(8,128)(2,1)S(1)}, u32[]{:S(2)}, u32[]{:S(2)}) collective-permute-start(bf16[32,1024]{1,0:T(8,128)(2,1)S(1)} %get-tuple-element.76), channel_id=1, source_target_pairs={{0,2},{1,3},{2,0},{3,1},{4,6},{5,7},{6,4},{7,5},{8,10},{9,11},{10,... | collective-permute-start | bytes 196616 | tf_op jit(solution)/shard_map/ppermute | solution.py:37
  80.4 9.0 %collective-permute-start.27 = (bf16[32,1024]{1,0:T(8,128)(2,1)S(1)}, bf16[32,1024]{1,0:T(8,128)(2,1)S(1)}, u32[]{:S(2)}, u32[]{:S(2)}) collective-permute-start(bf16[32,1024]{1,0:T(8,128)(2,1)S(1)} %get-tuple-element.77), channel_id=1, source_target_pairs={{0,3},{1,2},{2,1},{3,0},{4,7},{5,6},{6,5},{7,4},{8,11},{9,10},{10,... | collective-permute-start | bytes 196616 | tf_op jit(solution)/shard_map/ppermute | solution.py:37
  82.3 9.2 %collective-permute-start.29 = (bf16[32,1024]{1,0:T(8,128)(2,1)S(1)}, bf16[32,1024]{1,0:T(8,128)(2,1)S(1)}, u32[]{:S(2)}, u32[]{:S(2)}) collective-permute-start(bf16[32,1024]{1,0:T(8,128)(2,1)S(1)} %add_parts.9), channel_id=1, source_target_pairs={{0,2},{1,3},{2,0},{3,1},{4,6},{5,7},{6,4},{7,5},{8,10},{9,11},{10,... | collective-permute-start | bytes 196616 | tf_op jit(solution)/shard_map/ppermute | solution.py:37
  (12 other events, 359.2 us)
where the time goes:
time: 92.5 us; the launch traced here: 92.3 us
  waiting for transfers between devices  36.9 us (40%)
  starting transfers between devices  31.6 us (34%)
  Pallas kernels  22.4 us (24%)
  local copies, waits for them, and re-layouts  0.97 us (1%)
    ppermute x23, waiting for transfers between devices, exchange(): lax.ppermute(x, axis, [(i, i ^ bit) for i in range(lax.axis_size(axis))])  25.5 us
    ppermute x23, starting transfers between devices, exchange(): lax.ppermute(x, axis, [(i, i ^ bit) for i in range(lax.axis_size(axis))])  21 us
    ppermute x8, waiting for transfers between devices, shift(): return lax.ppermute(x, axis, [(i, (i + d) % n) for i in range(n)])  11.4 us
    ppermute x8, starting transfers between devices, shift(): return lax.ppermute(x, axis, [(i, (i + d) % n) for i in range(n)])  10.5 us
    pallas_call x3, Pallas kernels, load(): pl.pallas_call(kernel, name=name, out_shape=work.shapes + [jax.ShapeDtype...  9.7 us
    pallas_call x3, Pallas kernels, widen(): pl.pallas_call(kernel, name='widen', out_shape=[jax.ShapeDtypeStruct((hal...  4.58 us
    pallas_call x2, Pallas kernels, multiply(): pl.pallas_call(kernel, name=name, out_shape=[jax.ShapeDtypeStruct((share,...  3.36 us
    pallas_call x1, Pallas kernels, attend(): pl.pallas_call(kernel, name='attend', out_shape=jax.ShapeDtypeStruct((STE...  2.9 us
  transfers between devices with their start and end apart: 31, of which 19 were waited for; matrix products, arithmetic and copies ran while one was open for 0% of the time, Pallas kernels for 13%

commit v1 on v0

--- a/solution.py
+++ b/solution.py
@@ -82,22 +82,15 @@
             whole[pl.ds(at, rows), columns] = ref[d * rows : (d + 1) * rows, :]
 
 
-def reduce_ffn(own, near, keep, far, *ahead):
-    direct = [exchange(rows, "ffn", k + 2) for k, rows in enumerate(ahead)]
-    sums = add_parts(keep, exchange(far, "ffn", 1), len(ahead) // 2)
-    across = [exchange(part, "ffn", 2 * (k + 1)) for k, part in enumerate(sums)]
-    return [own, *direct, *across, exchange(near, "ffn", 1)]
+def reduce_ffn(own, *others):
+    masks = list(range(2, len(others) + 1)) + [1]
+    return [own] + [exchange(others[mask - 1], "ffn", mask) for mask in masks]
 
 
 def add_terms(refs, columns):
-    own, rest, near = refs[0], refs[1:-1], refs[-1]
-    half = own.shape[1] // 2
-    direct = 2 * len(rest) // 3
-    left = columns.stop <= half
-    total = own[:, columns] + near[:, columns].astype(F32)
-    here = columns if left else slice(columns.start - half, columns.stop - half)
-    for term in rest[:direct] if left else rest[direct:]:
-        total = total + term[:, here].astype(F32)
+    total = refs[0][:, columns]
+    for term in refs[1:]:
+        total = total + term[:, columns].astype(F32)
     return total
 
 
@@ -309,40 +302,26 @@
 
 def multiply(rows, w, name):
     columns = w.shape[1]
-    half = columns // 2
     count, depth = rows.shape
     ffn = lax.axis_size("ffn")
     share = count // ffn
-    rest = (ffn // 2 - 1) * share
-    block = min(512, half)
-
-    def kernel(rows, w, own, near, keep, far, *ahead):
-        for at in range(0, columns, block):
-            here = slice(at, at + block)
+    block = min(512, columns)
+
+    def kernel(rows, w, *outs):
+        for j in range(columns // block):
+            here = slice(j * block, (j + 1) * block)
             product = dot(rows[...], w[:, here])
-            own[:, here] = product[:share]
-            near[:, here] = product[share : 2 * share].astype(BF16)
-            for r in range(2, ffn):
-                part = product[r * share : (r + 1) * share]
-                if at < half:
-                    ahead[r - 2][:, here] = part.astype(BF16)
-                else:
-                    out = far if r % 2 else keep
-                    place = slice((r // 2 - 1) * share, r // 2 * share)
-                    out[place, at - half : at - half + block] = part.astype(out.dtype)
+            for r, out in enumerate(outs):
+                out[:, here] = product[r * share : (r + 1) * share].astype(out.dtype)
 
     return pl.pallas_call(
         kernel,
         name=name,
         out_shape=[
-            jax.ShapeDtypeStruct((share, columns), F32),
-            jax.ShapeDtypeStruct((share, columns), BF16),
-            jax.ShapeDtypeStruct((rest, half), F32),
-            jax.ShapeDtypeStruct((rest, half), BF16),
-        ]
-        + [jax.ShapeDtypeStruct((share, half), BF16)] * (ffn - 2),
+            jax.ShapeDtypeStruct((share, columns), BF16 if r else F32) for r in range(ffn)
+        ],
         in_specs=[VMEM] * 2,
-        out_specs=[VMEM] * (ffn + 2),
+        out_specs=[VMEM] * ffn,
         compiler_params=limit(4),
         cost_estimate=matmul_cost(count, depth, columns),
     )(rows, vmem(w))

time: 92.5 us -> 93.3 us (level)
  waiting for transfers between devices: 36.9 us -> 40.9 us
  starting transfers between devices: 31.6 us -> 28.4 us
    ppermute x23 -> x19, waiting for transfers between devices: 25.5 us -> 29.5 us  [exchange(): lax.ppermute(x, axis, [(i, i ^ bit) for i in range(lax.axis_size(axis))])]
    ppermute x23 -> x19, starting transfers between devices: 21 us -> 17.8 us  [exchange(): lax.ppermute(x, axis, [(i, i ^ bit) for i in range(lax.axis_size(axis))])]
  transfers between devices with their start and end apart: 31 -> 27, of which waited for: 19 -> 17; matrix products, arithmetic and copies ran while one was open for 0% -> 0% of each run, Pallas kernels for 13% -> 13%
where the time goes in v1:
time: 93.3 us; the launch traced here: 93.1 us
  waiting for transfers between devices  40.9 us (44%)
  starting transfers between devices  28.4 us (30%)
  Pallas kernels  22.4 us (24%)
  local copies, waits for them, and re-layouts  0.97 us (1%)
    ppermute x19, waiting for transfers between devices, exchange(): lax.ppermute(x, axis, [(i, i ^ bit) for i in range(lax.axis_size(axis))])  29.5 us
    ppermute x19, starting transfers between devices, exchange(): lax.ppermute(x, axis, [(i, i ^ bit) for i in range(lax.axis_size(axis))])  17.8 us
    ppermute x8, waiting for transfers between devices, shift(): return lax.ppermute(x, axis, [(i, (i + d) % n) for i in range(n)])  11.4 us
    ppermute x8, starting transfers between devices, shift(): return lax.ppermute(x, axis, [(i, (i + d) % n) for i in range(n)])  10.6 us
    pallas_call x3, Pallas kernels, load(): pl.pallas_call(kernel, name=name, out_shape=work.shapes + [jax.ShapeDtype...  9.7 us
    pallas_call x3, Pallas kernels, widen(): pl.pallas_call(kernel, name='widen', out_shape=[jax.ShapeDtypeStruct((hal...  4.57 us
    pallas_call x2, Pallas kernels, multiply(): pl.pallas_call(kernel, name=name, out_shape=[jax.ShapeDtypeStruct((share,...  3.36 us
    pallas_call x1, Pallas kernels, attend(): pl.pallas_call(kernel, name='attend', out_shape=jax.ShapeDtypeStruct((STE...  2.9 us
  transfers between devices with their start and end apart: 27, of which 17 were waited for; matrix products, arithmetic and copies ran while one was open for 0% of the time, Pallas kernels for 13%

profile of v1, /device:TPU:0, one launch (start us, length us, event | category | flops | bytes accessed | tf_op | source)
XLA Modules:
  0.0 93.1 jit_solution(15840649813865797222)
XLA Ops:
  0.0 1.6 %load_new.1 = (bf16[16,2,2048]{2,1,0:T(2,128)(2,1)S(1)}, bf16[16,2,512]{2,1,0:T(2,128)(2,1)S(1)}, f32[8,128]{1,0:T(8,128)}) custom-call(bf16[16,2,2048]{2,1,0:T(2,128)(2,1)} %refs_0_.3, bf16[16,2,512]{2,1,0:T(2,128)(2,1)} %refs_1_.1), custom_call_target="tpu_custom_call" | custom-call | bytes 327680 | tf_op jit(solution)/shard_map/load_new/pallas_call | solution.py:153
  1.7 3.0 %collective-permute-start = (bf16[16,5120]{1,0:T(8,128)(2,1)S(1)}, bf16[16,5120]{1,0:T(8,128)(2,1)S(1)}, u32[]{:S(2)}, u32[]{:S(2)}) collective-permute-start(bf16[16,5120]{1,0:T(8,128)(2,1)S(1)} %constant_dynamic-update-slice_fusion.refs_0_), channel_id=1, source_target_pairs={{0,8},{4,12},{8,0},{12,4},{1,9},{5,13},{9,1},{13,5},{2,10},{6,14},... | collective-permute-start | bytes 491528 | tf_op jit(solution)/shard_map/ppermute | solution.py:33
  4.8 4.4 %load_cache.1 = (bf16[16,640,512]{2,1,0:T(8,128)(2,1)S(1)}, s32[1,64]{1,0:T(1,128)S(1)}, s32[1,16]{1,0:T(1,128)S(1)}, bf16[16,2,2048]{2,1,0:T(2,128)(2,1)S(1)}, f32[8,128]{1,0:T(8,128)S(1)}) custom-call(bf16[16,640,512]{2,1,0:T(8,128)(2,1)} %refs_0_.4, s32[1,64]{1,0:T(1,128)} %bitcast.28, s32[1,16]{1,0:T(1,128)} %bitcast.29, bf16[64,2,2048]{2,1,0:T(2,128)(2,1)} %refs_3_.1, ...), custom_call_target="tpu_custom_call" | custom-call | bytes 21234304 | tf_op jit(solution)/shard_map/load_cache/pallas_call | solution.py:153
  9.3 1.6 %collective-permute-done.1.other = bf16[32,5120]{1,0:T(8,128)(2,1)S(1)} collective-permute-done((bf16[32,5120]{1,0:T(8,128)(2,1)S(1)}, bf16[32,5120]{1,0:T(8,128)(2,1)S(1)}, u32[]{:S(2)}, u32[]{:S(2)}) %collective-permute-start.1) | collective-permute-done | bytes 327712 | tf_op jit(solution)/shard_map/ppermute | solution.py:37
  11.0 2.9 %attend.1.refs_0_ = bf16[32,2048]{1,0:T(8,128)(2,1)S(1)} custom-call(s32[1,16]{1,0:T(1,128)S(1)} %get-tuple-element.42.lengths, s32[1,64]{1,0:T(1,128)S(1)} %get-tuple-element.41.slot_row, bf16[32,5120]{1,0:T(8,128)(2,1)S(1)} %join.5.same, bf16[32,5120]{1,0:T(8,128)(2,1)S(1)} %collective-permute-done.1.other, bf16[16,640,512]{2,1,0:T(8,128)(2,1)S(1)} %get-tuple-element.45.cache), custom_call_target="tpu_custom_call" | custom-call | flops 671088640 | bytes 10485760 | tf_op jit(solution)/shard_map/attend/pallas_call | solution.py:235
  13.9 1.5 %collective-permute-start.2 = (bf16[32,2048]{1,0:T(8,128)(2,1)S(1)}, bf16[32,2048]{1,0:T(8,128)(2,1)S(1)}, u32[]{:S(2)}, u32[]{:S(2)}) collective-permute-start(bf16[32,2048]{1,0:T(8,128)(2,1)S(1)} %attend.1.refs_0_), channel_id=1, source_target_pairs={{0,8},{4,12},{8,0},{12,4},{1,9},{5,13},{9,1},{13,5},{2,10},{6,14},... | collective-permute-start | bytes 393224 | tf_op jit(solution)/shard_map/ppermute | solution.py:33
  15.4 3.6 %load_out.1 = (bf16[2048,2048]{1,0:T(8,128)(2,1)S(1)}, f32[8,128]{1,0:T(8,128)S(1)}) custom-call(bf16[2048,2048]{1,0:T(8,128)(2,1)} %refs_0_.5, bf16[8,128]{1,0:T(8,128)(2,1)S(1)} %slice.17.refs_1_), custom_call_target="tpu_custom_call" | custom-call | bytes 16777216 | tf_op jit(solution)/shard_map/load_out/pallas_call | solution.py:153
  19.6 1.5 %collective-permute-done.3.other = bf16[64,2048]{1,0:T(8,128)(2,1)S(1)} collective-permute-done((bf16[64,2048]{1,0:T(8,128)(2,1)S(1)}, bf16[64,2048]{1,0:T(8,128)(2,1)S(1)}, u32[]{:S(2)}, u32[]{:S(2)}) %collective-permute-start.3) | collective-permute-done | bytes 262176 | tf_op jit(solution)/shard_map/ppermute | solution.py:37
  21.5 1.3 %project.1 = (f32[32,2048]{1,0:T(8,128)S(1)}, bf16[32,2048]{1,0:T(8,128)(2,1)S(1)}, bf16[32,2048]{1,0:T(8,128)(2,1)S(1)}, bf16[32,2048]{1,0:T(8,128)(2,1)S(1)}) custom-call(bf16[128,2048]{1,0:T(8,128)(2,1)S(1)} %order_rows.1.rows, bf16[2048,2048]{1,0:T(8,128)(2,1)S(1)} %get-tuple-element.47.w), custom_call_target="tpu_custom_call" | custom-call | flops 1073741824 | bytes 9437184 | tf_op jit(solution)/shard_map/project/pallas_call | solution.py:317
  22.8 2.7 %collective-permute-start.4 = (bf16[32,2048]{1,0:T(8,128)(2,1)S(1)}, bf16[32,2048]{1,0:T(8,128)(2,1)S(1)}, u32[]{:S(2)}, u32[]{:S(2)}) collective-permute-start(bf16[32,2048]{1,0:T(8,128)(2,1)S(1)} %get-tuple-element.49), channel_id=1, source_target_pairs={{0,2},{1,3},{2,0},{3,1},{4,6},{5,7},{6,4},{7,5},{8,10},{9,11},{10,... | collective-permute-start | bytes 393224 | tf_op jit(solution)/shard_map/ppermute | solution.py:37
  25.5 1.3 %collective-permute-start.5 = (bf16[32,2048]{1,0:T(8,128)(2,1)S(1)}, bf16[32,2048]{1,0:T(8,128)(2,1)S(1)}, u32[]{:S(2)}, u32[]{:S(2)}) collective-permute-start(bf16[32,2048]{1,0:T(8,128)(2,1)S(1)} %get-tuple-element.50), channel_id=1, source_target_pairs={{0,3},{1,2},{2,1},{3,0},{4,7},{5,6},{6,5},{7,4},{8,11},{9,10},{10,... | collective-permute-start | bytes 393224 | tf_op jit(solution)/shard_map/ppermute | solution.py:37
  27.1 8.7 %collective-permute-done.4.refs_1_ = bf16[32,2048]{1,0:T(8,128)(2,1)S(1)} collective-permute-done((bf16[32,2048]{1,0:T(8,128)(2,1)S(1)}, bf16[32,2048]{1,0:T(8,128)(2,1)S(1)}, u32[]{:S(2)}, u32[]{:S(2)}) %collective-permute-start.4) | collective-permute-done | bytes 131104 | tf_op jit(solution)/shard_map/ppermute | solution.py:37
  36.4 4.1 %collective-permute-start.8 = (bf16[32,1024]{1,0:T(8,128)(2,1)S(1)}, bf16[32,1024]{1,0:T(8,128)(2,1)S(1)}, u32[]{:S(2)}, u32[]{:S(2)}) collective-permute-start(bf16[32,1024]{1,0:T(8,128)(2,1)S(1)} %get-tuple-element.53), channel_id=1, source_target_pairs={{0,2},{1,3},{2,0},{3,1},{4,6},{5,7},{6,4},{7,5},{8,10},{9,11},{10,... | collective-permute-start | bytes 196616 | tf_op jit(solution)/shard_map/ppermute | solution.py:37
  40.6 1.0 %collective-permute-start.11 = (bf16[32,1024]{1,0:T(8,128)(2,1)S(1)}, bf16[32,1024]{1,0:T(8,128)(2,1)S(1)}, u32[]{:S(2)}, u32[]{:S(2)}) collective-permute-start(bf16[32,1024]{1,0:T(8,128)(2,1)S(1)} %get-tuple-element.54), channel_id=1, source_target_pairs={{0,2},{1,3},{2,0},{3,1},{4,6},{5,7},{6,4},{7,5},{8,10},{9,11},{10,... | collective-permute-start | bytes 196616 | tf_op jit(solution)/shard_map/ppermute | solution.py:37
  41.6 3.4 %collective-permute-start.10 = (bf16[32,1024]{1,0:T(8,128)(2,1)S(1)}, bf16[32,1024]{1,0:T(8,128)(2,1)S(1)}, u32[]{:S(2)}, u32[]{:S(2)}) collective-permute-start(bf16[32,1024]{1,0:T(8,128)(2,1)S(1)} %get-tuple-element.54), channel_id=1, source_target_pairs={{0,3},{1,2},{2,1},{3,0},{4,7},{5,6},{6,5},{7,4},{8,11},{9,10},{10,... | collective-permute-start | bytes 196616 | tf_op jit(solution)/shard_map/ppermute | solution.py:37
  44.9 4.0 %collective-permute-done.11.refs_4_ = bf16[32,1024]{1,0:T(8,128)(2,1)S(1)} collective-permute-done((bf16[32,1024]{1,0:T(8,128)(2,1)S(1)}, bf16[32,1024]{1,0:T(8,128)(2,1)S(1)}, u32[]{:S(2)}, u32[]{:S(2)}) %collective-permute-start.11) | collective-permute-done | bytes 65568 | tf_op jit(solution)/shard_map/ppermute | solution.py:37
  51.2 1.3 %widen.3 = (bf16[64,2176]{1,0:T(8,128)(2,1)S(1)}, bf16[64,2176]{1,0:T(8,128)(2,1)S(1)}) custom-call(bf16[128,2048]{1,0:T(8,128)(2,1)S(1)} %get-tuple-element.55.normed, bf16[128,128]{1,0:T(8,128)(2,1)S(1)} %get-tuple-element.56.tail, bf16[2048,3584]{1,0:T(8,128)(2,1)S(1)} %bitcast.14, bf16[2048,3584]{1,0:T(8,128)(2,1)S(1)} %bitcast.16), custom_call_target="tpu_custom_call" | custom-call | flops 1073741824 | bytes 9437184 | tf_op jit(solution)/shard_map/widen/pallas_call | solution.py:433
  52.6 1.9 %widen.4 = (bf16[64,3200]{1,0:T(8,128)(2,1)S(1)}, bf16[64,3200]{1,0:T(8,128)(2,1)S(1)}) custom-call(bf16[128,2048]{1,0:T(8,128)(2,1)S(1)} %get-tuple-element.55.normed, bf16[128,128]{1,0:T(8,128)(2,1)S(1)} %get-tuple-element.56.tail, bf16[2048,3584]{1,0:T(8,128)(2,1)S(1)} %bitcast.14, bf16[2048,3584]{1,0:T(8,128)(2,1)S(1)} %bitcast.16, ...), custom_call_target="tpu_custom_call" | custom-call | flops 1610612736 | bytes 13893632 | tf_op jit(solution)/shard_map/widen/pallas_call | solution.py:433
  55.2 1.5 %collective-permute-start.13 = (bf16[32,2176]{1,0:T(8,128)(2,1)S(1)}, bf16[32,2176]{1,0:T(8,128)(2,1)S(1)}, u32[]{:S(2)}, u32[]{:S(2)}) collective-permute-start(bf16[32,2176]{1,0:T(8,128)(2,1)S(1)} %get-tuple-element.60), channel_id=1, source_target_pairs={{0,8},{4,12},{8,0},{12,4},{1,9},{5,13},{9,1},{13,5},{2,10},{6,14},... | collective-permute-start | bytes 417800 | tf_op jit(solution)/shard_map/ppermute | solution.py:33
  56.7 1.3 %widen.5 = (bf16[64,2176]{1,0:T(8,128)(2,1)S(1)}, bf16[64,2176]{1,0:T(8,128)(2,1)S(1)}) custom-call(bf16[128,2048]{1,0:T(8,128)(2,1)S(1)} %get-tuple-element.55.normed, bf16[128,128]{1,0:T(8,128)(2,1)S(1)} %get-tuple-element.56.tail, bf16[2048,3584]{1,0:T(8,128)(2,1)S(1)} %bitcast.14, bf16[2048,3584]{1,0:T(8,128)(2,1)S(1)} %bitcast.16, ...), custom_call_target="tpu_custom_call" | custom-call | flops 1073741824 | bytes 9437184 | tf_op jit(solution)/shard_map/widen/pallas_call | solution.py:433
  58.9 2.0 %collective-permute-done.13.refs_1_ = bf16[32,2176]{1,0:T(8,128)(2,1)S(1)} collective-permute-done((bf16[32,2176]{1,0:T(8,128)(2,1)S(1)}, bf16[32,2176]{1,0:T(8,128)(2,1)S(1)}, u32[]{:S(2)}, u32[]{:S(2)}) %collective-permute-start.13) | collective-permute-done | bytes 139296 | tf_op jit(solution)/shard_map/ppermute | solution.py:33
  61.1 1.8 %collective-permute-start.14 = (bf16[32,1024]{1,0:T(8,128)(2,1)S(1)}, bf16[32,1024]{1,0:T(8,128)(2,1)S(1)}, u32[]{:S(2)}, u32[]{:S(2)}) collective-permute-start(bf16[32,1024]{1,0:T(8,128)(2,1)S(1)} %gate.7.refs_0_), channel_id=1, source_target_pairs={{0,8},{4,12},{8,0},{12,4},{1,9},{5,13},{9,1},{13,5},{2,10},{6,14},... | collective-permute-start | bytes 196616 | tf_op jit(solution)/shard_map/ppermute | solution.py:33
  63.3 2.9 %collective-permute-done.17.refs_1_ = bf16[32,3200]{1,0:T(8,128)(2,1)S(1)} collective-permute-done((bf16[32,3200]{1,0:T(8,128)(2,1)S(1)}, bf16[32,3200]{1,0:T(8,128)(2,1)S(1)}, u32[]{:S(2)}, u32[]{:S(2)}) %collective-permute-start.17) | collective-permute-done | bytes 204832 | tf_op jit(solution)/shard_map/ppermute | solution.py:33
  66.4 0.9 collective-permute-start.18
  67.3 3.3 %collective-permute-done.21.refs_1_ = bf16[32,2176]{1,0:T(8,128)(2,1)S(1)} collective-permute-done((bf16[32,2176]{1,0:T(8,128)(2,1)S(1)}, bf16[32,2176]{1,0:T(8,128)(2,1)S(1)}, u32[]{:S(2)}, u32[]{:S(2)}) %collective-permute-start.21) | collective-permute-done | bytes 139296 | tf_op jit(solution)/shard_map/ppermute | solution.py:33
  70.8 0.9 collective-permute-start.22
  72.9 2.1 %collective-permute-done.22.refs_1_ = bf16[32,1024]{1,0:T(8,128)(2,1)S(1)} collective-permute-done((bf16[32,1024]{1,0:T(8,128)(2,1)S(1)}, bf16[32,1024]{1,0:T(8,128)(2,1)S(1)}, u32[]{:S(2)}, u32[]{:S(2)}) %collective-permute-start.22) | collective-permute-done | bytes 65568 | tf_op jit(solution)/shard_map/ppermute | solution.py:33
  75.2 1.3 %collective-permute-done.23.refs_5_ = bf16[64,1024]{1,0:T(8,128)(2,1)S(1)} collective-permute-done((bf16[64,1024]{1,0:T(8,128)(2,1)S(1)}, bf16[64,1024]{1,0:T(8,128)(2,1)S(1)}, u32[]{:S(2)}, u32[]{:S(2)}) %collective-permute-start.23) | collective-permute-done | bytes 131104 | tf_op jit(solution)/shard_map/ppermute | solution.py:37
  76.7 2.1 %narrow.1 = (f32[32,2048]{1,0:T(8,128)S(1)}, bf16[32,2048]{1,0:T(8,128)(2,1)S(1)}, bf16[32,2048]{1,0:T(8,128)(2,1)S(1)}, bf16[32,2048]{1,0:T(8,128)(2,1)S(1)}) custom-call(bf16[128,3584]{1,0:T(8,128)(2,1)S(1)} %place_rows.1.rows, bf16[3584,2048]{1,0:T(8,128)(2,1)S(1)} %bitcast.18), custom_call_target="tpu_custom_call" | custom-call | flops 1879048192 | bytes 16121856 | tf_op jit(solution)/shard_map/narrow/pallas_call | solution.py:317
  78.9 3.1 %collective-permute-start.25 = (bf16[32,2048]{1,0:T(8,128)(2,1)S(1)}, bf16[32,2048]{1,0:T(8,128)(2,1)S(1)}, u32[]{:S(2)}, u32[]{:S(2)}) collective-permute-start(bf16[32,2048]{1,0:T(8,128)(2,1)S(1)} %get-tuple-element.71), channel_id=1, source_target_pairs={{0,3},{1,2},{2,1},{3,0},{4,7},{5,6},{6,5},{7,4},{8,11},{9,10},{10,... | collective-permute-start | bytes 393224 | tf_op jit(solution)/shard_map/ppermute | solution.py:37
  82.3 9.0 %collective-permute-done.24.refs_1_ = bf16[32,2048]{1,0:T(8,128)(2,1)S(1)} collective-permute-done((bf16[32,2048]{1,0:T(8,128)(2,1)S(1)}, bf16[32,2048]{1,0:T(8,128)(2,1)S(1)}, u32[]{:S(2)}, u32[]{:S(2)}) %collective-permute-start.24) | collective-permute-done | bytes 131104 | tf_op jit(solution)/shard_map/ppermute | solution.py:37
  91.3 1.0 %collective-permute-done.26.refs_3_ = bf16[32,2048]{1,0:T(8,128)(2,1)S(1)} collective-permute-done((bf16[32,2048]{1,0:T(8,128)(2,1)S(1)}, bf16[32,2048]{1,0:T(8,128)(2,1)S(1)}, u32[]{:S(2)}, u32[]{:S(2)}) %collective-permute-start.26) | collective-permute-done | bytes 131104 | tf_op jit(solution)/shard_map/ppermute | solution.py:37
  (86 shorter events, 9.5 us)
Async XLA Ops:
  1.7 7.5 %collective-permute-start = (bf16[16,5120]{1,0:T(8,128)(2,1)S(1)}, bf16[16,5120]{1,0:T(8,128)(2,1)S(1)}, u32[]{:S(2)}, u32[]{:S(2)}) collective-permute-start(bf16[16,5120]{1,0:T(8,128)(2,1)S(1)} %constant_dynamic-update-slice_fusion.refs_0_), channel_id=1, source_target_pairs={{0,8},{4,12},{8,0},{12,4},{1,9},{5,13},{9,1},{13,5},{2,10},{6,14},... | collective-permute-start | bytes 491528 | tf_op jit(solution)/shard_map/ppermute | solution.py:33
  4.8 46.4 %slice-start.4 = ((s8[14680064]{0:T(1024)(128)(4,1)}), s8[4194304]{0:T(1024)(128)(4,1)S(1)}, s32[]{:S(2)}) async-start(s8[14680064]{0:T(1024)(128)(4,1)} %bitcast.15), calls=%async_computation.4 | async-start | bytes 8388608
  4.8 46.4 %slice-start.5 = ((s8[14680064]{0:T(1024)(128)(4,1)}), s8[4194304]{0:T(1024)(128)(4,1)S(1)}, s32[]{:S(2)}) async-start(s8[14680064]{0:T(1024)(128)(4,1)} %bitcast.15), calls=%async_computation.5 | async-start | bytes 8388608
  9.3 1.7 %collective-permute-start.1 = (bf16[32,5120]{1,0:T(8,128)(2,1)S(1)}, bf16[32,5120]{1,0:T(8,128)(2,1)S(1)}, u32[]{:S(2)}, u32[]{:S(2)}) collective-permute-start(bf16[32,5120]{1,0:T(8,128)(2,1)S(1)} %join.5.same), channel_id=1, source_target_pairs={{0,4},{4,0},{8,12},{12,8},{1,5},{5,1},{9,13},{13,9},{2,6},{6,2},{1... | collective-permute-start | bytes 983048 | tf_op jit(solution)/shard_map/ppermute | solution.py:37
  10.9 40.2 %slice-start = ((s8[14680064]{0:T(1024)(128)(4,1)}), s8[4194304]{0:T(1024)(128)(4,1)S(1)}, s32[]{:S(2)}) async-start(s8[14680064]{0:T(1024)(128)(4,1)} %bitcast.13), calls=%async_computation | async-start | bytes 8388608
  10.9 40.2 %slice-start.1 = ((s8[14680064]{0:T(1024)(128)(4,1)}), s8[4194304]{0:T(1024)(128)(4,1)S(1)}, s32[]{:S(2)}) async-start(s8[14680064]{0:T(1024)(128)(4,1)} %bitcast.13), calls=%async_computation.1 | async-start | bytes 8388608
  11.0 40.2 %slice-start.6 = ((s8[14680064]{0:T(1024)(128)(4,1)}), s8[4194304]{0:T(1024)(128)(4,1)S(1)}, s32[]{:S(2)}) async-start(s8[14680064]{0:T(1024)(128)(4,1)} %bitcast.15), calls=%async_computation.6 | async-start | bytes 8388608
  13.9 5.6 %collective-permute-start.2 = (bf16[32,2048]{1,0:T(8,128)(2,1)S(1)}, bf16[32,2048]{1,0:T(8,128)(2,1)S(1)}, u32[]{:S(2)}, u32[]{:S(2)}) collective-permute-start(bf16[32,2048]{1,0:T(8,128)(2,1)S(1)} %attend.1.refs_0_), channel_id=1, source_target_pairs={{0,8},{4,12},{8,0},{12,4},{1,9},{5,13},{9,1},{13,5},{2,10},{6,14},... | collective-permute-start | bytes 393224 | tf_op jit(solution)/shard_map/ppermute | solution.py:33
  19.5 1.6 %collective-permute-start.3 = (bf16[64,2048]{1,0:T(8,128)(2,1)S(1)}, bf16[64,2048]{1,0:T(8,128)(2,1)S(1)}, u32[]{:S(2)}, u32[]{:S(2)}) collective-permute-start(bf16[64,2048]{1,0:T(8,128)(2,1)S(1)} %join.6.same), channel_id=1, source_target_pairs={{0,4},{4,0},{8,12},{12,8},{1,5},{5,1},{9,13},{13,9},{2,6},{6,2},{1... | collective-permute-start | bytes 786440 | tf_op jit(solution)/shard_map/ppermute | solution.py:37
  22.8 13.0 %collective-permute-start.4 = (bf16[32,2048]{1,0:T(8,128)(2,1)S(1)}, bf16[32,2048]{1,0:T(8,128)(2,1)S(1)}, u32[]{:S(2)}, u32[]{:S(2)}) collective-permute-start(bf16[32,2048]{1,0:T(8,128)(2,1)S(1)} %get-tuple-element.49), channel_id=1, source_target_pairs={{0,2},{1,3},{2,0},{3,1},{4,6},{5,7},{6,4},{7,5},{8,10},{9,11},{10,... | collective-permute-start | bytes 393224 | tf_op jit(solution)/shard_map/ppermute | solution.py:37
  25.5 10.3 %collective-permute-start.5 = (bf16[32,2048]{1,0:T(8,128)(2,1)S(1)}, bf16[32,2048]{1,0:T(8,128)(2,1)S(1)}, u32[]{:S(2)}, u32[]{:S(2)}) collective-permute-start(bf16[32,2048]{1,0:T(8,128)(2,1)S(1)} %get-tuple-element.50), channel_id=1, source_target_pairs={{0,3},{1,2},{2,1},{3,0},{4,7},{5,6},{6,5},{7,4},{8,11},{9,10},{10,... | collective-permute-start | bytes 393224 | tf_op jit(solution)/shard_map/ppermute | solution.py:37
  26.8 9.5 %collective-permute-start.6 = (bf16[32,2048]{1,0:T(8,128)(2,1)S(1)}, bf16[32,2048]{1,0:T(8,128)(2,1)S(1)}, u32[]{:S(2)}, u32[]{:S(2)}) collective-permute-start(bf16[32,2048]{1,0:T(8,128)(2,1)S(1)} %get-tuple-element.51), channel_id=1, source_target_pairs={{0,1},{1,0},{2,3},{3,2},{4,5},{5,4},{6,7},{7,6},{8,9},{9,8},{10,11... | collective-permute-start | bytes 393224 | tf_op jit(solution)/shard_map/ppermute | solution.py:37
  36.4 8.5 %collective-permute-start.8 = (bf16[32,1024]{1,0:T(8,128)(2,1)S(1)}, bf16[32,1024]{1,0:T(8,128)(2,1)S(1)}, u32[]{:S(2)}, u32[]{:S(2)}) collective-permute-start(bf16[32,1024]{1,0:T(8,128)(2,1)S(1)} %get-tuple-element.53), channel_id=1, source_target_pairs={{0,2},{1,3},{2,0},{3,1},{4,6},{5,7},{6,4},{7,5},{8,10},{9,11},{10,... | collective-permute-start | bytes 196616 | tf_op jit(solution)/shard_map/ppermute | solution.py:37
  40.5 9.4 %collective-permute-start.7 = (bf16[32,2048]{1,0:T(8,128)(2,1)S(1)}, bf16[32,2048]{1,0:T(8,128)(2,1)S(1)}, u32[]{:S(2)}, u32[]{:S(2)}) collective-permute-start(bf16[32,2048]{1,0:T(8,128)(2,1)S(1)} %get-tuple-element.52.refs_5_.residual), channel_id=1, source_target_pairs={{0,1},{1,0},{2,3},{3,2},{4,5},{5,4},{6,7},{7,6},{8,9},{9,8},{10,11... | collective-permute-start | bytes 393224 | tf_op jit(solution)/shard_map/ppermute | solution.py:37
  40.6 8.4 %collective-permute-start.11 = (bf16[32,1024]{1,0:T(8,128)(2,1)S(1)}, bf16[32,1024]{1,0:T(8,128)(2,1)S(1)}, u32[]{:S(2)}, u32[]{:S(2)}) collective-permute-start(bf16[32,1024]{1,0:T(8,128)(2,1)S(1)} %get-tuple-element.54), channel_id=1, source_target_pairs={{0,2},{1,3},{2,0},{3,1},{4,6},{5,7},{6,4},{7,5},{8,10},{9,11},{10,... | collective-permute-start | bytes 196616 | tf_op jit(solution)/shard_map/ppermute | solution.py:37
  41.6 7.9 %collective-permute-start.10 = (bf16[32,1024]{1,0:T(8,128)(2,1)S(1)}, bf16[32,1024]{1,0:T(8,128)(2,1)S(1)}, u32[]{:S(2)}, u32[]{:S(2)}) collective-permute-start(bf16[32,1024]{1,0:T(8,128)(2,1)S(1)} %get-tuple-element.54), channel_id=1, source_target_pairs={{0,3},{1,2},{2,1},{3,0},{4,7},{5,6},{6,5},{7,4},{8,11},{9,10},{10,... | collective-permute-start | bytes 196616 | tf_op jit(solution)/shard_map/ppermute | solution.py:37
  44.9 5.9 %collective-permute-start.9 = (bf16[32,1024]{1,0:T(8,128)(2,1)S(1)}, bf16[32,1024]{1,0:T(8,128)(2,1)S(1)}, u32[]{:S(2)}, u32[]{:S(2)}) collective-permute-start(bf16[32,1024]{1,0:T(8,128)(2,1)S(1)} %collective-permute-done.8.refs_2_), channel_id=1, source_target_pairs={{0,1},{1,0},{2,3},{3,2},{4,5},{5,4},{6,7},{7,6},{8,9},{9,8},{10,11... | collective-permute-start | bytes 196616 | tf_op jit(solution)/shard_map/ppermute | solution.py:37
  52.5 2.6 %collective-permute-start.12 = (bf16[64,2176]{1,0:T(8,128)(2,1)S(1)}, bf16[64,2176]{1,0:T(8,128)(2,1)S(1)}, u32[]{:S(2)}, u32[]{:S(2)}) collective-permute-start(bf16[64,2176]{1,0:T(8,128)(2,1)S(1)} %get-tuple-element.58), channel_id=1, source_target_pairs={{0,4},{4,0},{8,12},{12,8},{1,5},{5,1},{9,13},{13,9},{2,6},{6,2},{1... | collective-permute-start | bytes 835592 | tf_op jit(solution)/shard_map/ppermute | solution.py:37
  54.5 3.6 %collective-permute-start.16 = (bf16[64,3200]{1,0:T(8,128)(2,1)S(1)}, bf16[64,3200]{1,0:T(8,128)(2,1)S(1)}, u32[]{:S(2)}, u32[]{:S(2)}) collective-permute-start(bf16[64,3200]{1,0:T(8,128)(2,1)S(1)} %get-tuple-element.62), channel_id=1, source_target_pairs={{0,4},{4,0},{8,12},{12,8},{1,5},{5,1},{9,13},{13,9},{2,6},{6,2},{1... | collective-permute-start | bytes 1228808 | tf_op jit(solution)/shard_map/ppermute | solution.py:37
  55.2 5.7 %collective-permute-start.13 = (bf16[32,2176]{1,0:T(8,128)(2,1)S(1)}, bf16[32,2176]{1,0:T(8,128)(2,1)S(1)}, u32[]{:S(2)}, u32[]{:S(2)}) collective-permute-start(bf16[32,2176]{1,0:T(8,128)(2,1)S(1)} %get-tuple-element.60), channel_id=1, source_target_pairs={{0,8},{4,12},{8,0},{12,4},{1,9},{5,13},{9,1},{13,5},{2,10},{6,14},... | collective-permute-start | bytes 417800 | tf_op jit(solution)/shard_map/ppermute | solution.py:33
  58.0 4.8 %collective-permute-start.20 = (bf16[64,2176]{1,0:T(8,128)(2,1)S(1)}, bf16[64,2176]{1,0:T(8,128)(2,1)S(1)}, u32[]{:S(2)}, u32[]{:S(2)}) collective-permute-start(bf16[64,2176]{1,0:T(8,128)(2,1)S(1)} %get-tuple-element.66), channel_id=1, source_target_pairs={{0,4},{4,0},{8,12},{12,8},{1,5},{5,1},{9,13},{13,9},{2,6},{6,2},{1... | collective-permute-start | bytes 835592 | tf_op jit(solution)/shard_map/ppermute | solution.py:37
  58.2 7.9 %collective-permute-start.17 = (bf16[32,3200]{1,0:T(8,128)(2,1)S(1)}, bf16[32,3200]{1,0:T(8,128)(2,1)S(1)}, u32[]{:S(2)}, u32[]{:S(2)}) collective-permute-start(bf16[32,3200]{1,0:T(8,128)(2,1)S(1)} %get-tuple-element.64), channel_id=1, source_target_pairs={{0,8},{4,12},{8,0},{12,4},{1,9},{5,13},{9,1},{13,5},{2,10},{6,14},... | collective-permute-start | bytes 614408 | tf_op jit(solution)/shard_map/ppermute | solution.py:33
  61.1 11.3 %collective-permute-start.14 = (bf16[32,1024]{1,0:T(8,128)(2,1)S(1)}, bf16[32,1024]{1,0:T(8,128)(2,1)S(1)}, u32[]{:S(2)}, u32[]{:S(2)}) collective-permute-start(bf16[32,1024]{1,0:T(8,128)(2,1)S(1)} %gate.7.refs_0_), channel_id=1, source_target_pairs={{0,8},{4,12},{8,0},{12,4},{1,9},{5,13},{9,1},{13,5},{2,10},{6,14},... | collective-permute-start | bytes 196616 | tf_op jit(solution)/shard_map/ppermute | solution.py:33
  62.9 7.6 %collective-permute-start.21 = (bf16[32,2176]{1,0:T(8,128)(2,1)S(1)}, bf16[32,2176]{1,0:T(8,128)(2,1)S(1)}, u32[]{:S(2)}, u32[]{:S(2)}) collective-permute-start(bf16[32,2176]{1,0:T(8,128)(2,1)S(1)} %get-tuple-element.68), channel_id=1, source_target_pairs={{0,8},{4,12},{8,0},{12,4},{1,9},{5,13},{9,1},{13,5},{2,10},{6,14},... | collective-permute-start | bytes 417800 | tf_op jit(solution)/shard_map/ppermute | solution.py:33
  66.4 5.9 %collective-permute-start.18 = (bf16[32,1536]{1,0:T(8,128)(2,1)S(1)}, bf16[32,1536]{1,0:T(8,128)(2,1)S(1)}, u32[]{:S(2)}, u32[]{:S(2)}) collective-permute-start(bf16[32,1536]{1,0:T(8,128)(2,1)S(1)} %gate.9.refs_0_), channel_id=1, source_target_pairs={{0,8},{4,12},{8,0},{12,4},{1,9},{5,13},{9,1},{13,5},{2,10},{6,14},... | collective-permute-start | bytes 294920 | tf_op jit(solution)/shard_map/ppermute | solution.py:33
  70.8 4.3 %collective-permute-start.22 = (bf16[32,1024]{1,0:T(8,128)(2,1)S(1)}, bf16[32,1024]{1,0:T(8,128)(2,1)S(1)}, u32[]{:S(2)}, u32[]{:S(2)}) collective-permute-start(bf16[32,1024]{1,0:T(8,128)(2,1)S(1)} %gate.11.refs_0_), channel_id=1, source_target_pairs={{0,8},{4,12},{8,0},{12,4},{1,9},{5,13},{9,1},{13,5},{2,10},{6,14},... | collective-permute-start | bytes 196616 | tf_op jit(solution)/shard_map/ppermute | solution.py:33
  72.3 4.2 %collective-permute-start.19 = (bf16[64,1536]{1,0:T(8,128)(2,1)S(1)}, bf16[64,1536]{1,0:T(8,128)(2,1)S(1)}, u32[]{:S(2)}, u32[]{:S(2)}) collective-permute-start(bf16[64,1536]{1,0:T(8,128)(2,1)S(1)} %join.8.refs_2_), channel_id=1, source_target_pairs={{0,4},{4,0},{8,12},{12,8},{1,5},{5,1},{9,13},{13,9},{2,6},{6,2},{1... | collective-permute-start | bytes 589832 | tf_op jit(solution)/shard_map/ppermute | solution.py:37
  72.4 2.8 %collective-permute-start.15 = (bf16[64,1024]{1,0:T(8,128)(2,1)S(1)}, bf16[64,1024]{1,0:T(8,128)(2,1)S(1)}, u32[]{:S(2)}, u32[]{:S(2)}) collective-permute-start(bf16[64,1024]{1,0:T(8,128)(2,1)S(1)} %join.7.refs_0_), channel_id=1, source_target_pairs={{0,4},{4,0},{8,12},{12,8},{1,5},{5,1},{9,13},{13,9},{2,6},{6,2},{1... | collective-permute-start | bytes 393224 | tf_op jit(solution)/shard_map/ppermute | solution.py:37
  75.1 1.4 %collective-permute-start.23 = (bf16[64,1024]{1,0:T(8,128)(2,1)S(1)}, bf16[64,1024]{1,0:T(8,128)(2,1)S(1)}, u32[]{:S(2)}, u32[]{:S(2)}) collective-permute-start(bf16[64,1024]{1,0:T(8,128)(2,1)S(1)} %join.9.refs_4_), channel_id=1, source_target_pairs={{0,4},{4,0},{8,12},{12,8},{1,5},{5,1},{9,13},{13,9},{2,6},{6,2},{1... | collective-permute-start | bytes 393224 | tf_op jit(solution)/shard_map/ppermute | solution.py:37
  78.7 12.5 %collective-permute-start.24 = (bf16[32,2048]{1,0:T(8,128)(2,1)S(1)}, bf16[32,2048]{1,0:T(8,128)(2,1)S(1)}, u32[]{:S(2)}, u32[]{:S(2)}) collective-permute-start(bf16[32,2048]{1,0:T(8,128)(2,1)S(1)} %get-tuple-element.70), channel_id=1, source_target_pairs={{0,2},{1,3},{2,0},{3,1},{4,6},{5,7},{6,4},{7,5},{8,10},{9,11},{10,... | collective-permute-start | bytes 393224 | tf_op jit(solution)/shard_map/ppermute | solution.py:37
  78.9 12.4 %collective-permute-start.25 = (bf16[32,2048]{1,0:T(8,128)(2,1)S(1)}, bf16[32,2048]{1,0:T(8,128)(2,1)S(1)}, u32[]{:S(2)}, u32[]{:S(2)}) collective-permute-start(bf16[32,2048]{1,0:T(8,128)(2,1)S(1)} %get-tuple-element.71), channel_id=1, source_target_pairs={{0,3},{1,2},{2,1},{3,0},{4,7},{5,6},{6,5},{7,4},{8,11},{9,10},{10,... | collective-permute-start | bytes 393224 | tf_op jit(solution)/shard_map/ppermute | solution.py:37
  82.0 10.2 %collective-permute-start.26 = (bf16[32,2048]{1,0:T(8,128)(2,1)S(1)}, bf16[32,2048]{1,0:T(8,128)(2,1)S(1)}, u32[]{:S(2)}, u32[]{:S(2)}) collective-permute-start(bf16[32,2048]{1,0:T(8,128)(2,1)S(1)} %get-tuple-element.72), channel_id=1, source_target_pairs={{0,1},{1,0},{2,3},{3,2},{4,5},{5,4},{6,7},{7,6},{8,9},{9,8},{10,11... | collective-permute-start | bytes 393224 | tf_op jit(solution)/shard_map/ppermute | solution.py:37
  (8 other events, 204.3 us)
